TPU v7x, 256 devices: a whole 4x4x8 slice. The times are simulated.
256 devices in a mesh: elem: 32 (over y_lo, z, core), state: 8 (over y_hi, x).
Axes of the slice: x: 4, y: 4 (y_hi: 2, y_lo: 2; y = y_hi * 2 + y_lo), z: 8, core: 2. Of those that a mesh axis runs over, the one named last changes fastest.
Arguments:
- coefficients: bfloat16 [2048, 64, 1024], P('elem', None, 'state'), may hold values from -1200 to 1200
- hamiltonian: bfloat16 [2048, 64, 448], P('elem'), may hold values from -0.25 to 0.25
- neighbours: int32 [2048, 6], P('elem'), may hold values from 0 to 2047, as said below
- pattern: int32 [2048, 6], P('elem'), may hold values 0 or 1
Outputs:
- orthonormal: bfloat16 [2048, 64, 1024], P('elem', None, 'state')
Inputs may be any that keep to these rules, and one draw needn't show every extreme that they name: Elements form layers of 32 consecutive ids, cyclically ordered; across face 0 lie the elements of the next layer, across face 1 those of the previous layer, across faces 2 to 5 those of the same layer; for each face, the neighbours of one layer's elements are all elements of the target layer, each once.
All inputs are finite; a program needn't handle non-finite values. No bound on the sum of `pattern` on one device may be relied on, other than what follows from the above.
Results may differ from a plain program's by a relative error of at most 0.0061.
Values may be sent and summed in bfloat16 or wider, within the bound.
A program may use at most 128 MiB of HBM per device.

v0:
```python
import jax
import jax.numpy as jnp
from jax import lax
from jax.sharding import PartitionSpec as P

NS = 1024
LAYER = 32


CENTER = 0.5
HALF_WIDTH = 2.0


def with_halo(cells, sides, width):
    for axis, dim in sides:
        count = lax.axis_size(axis)
        head = lax.slice_in_dim(cells, 0, width, axis=dim)
        tail = lax.slice_in_dim(cells, cells.shape[dim] - width, cells.shape[dim], axis=dim)
        cells = jnp.concatenate(
            [
                lax.ppermute(tail, axis, [(i, (i + 1) % count) for i in range(count)]),
                cells,
                lax.ppermute(head, axis, [((i + 1) % count, i) for i in range(count)]),
            ],
            axis=dim,
        )
    return cells


def apply_hamiltonian(coeffs, hamilton, slots, weights):
    padded = with_halo(coeffs, (("elem", 0),), LAYER)
    gathered = padded[slots] * weights
    stacked = jnp.concatenate([coeffs[:, None], gathered], axis=1)
    stacked = stacked.reshape(coeffs.shape[0], 7 * coeffs.shape[1], coeffs.shape[2])
    return jnp.einsum("eik,eks->eis", hamilton, stacked, preferred_element_type=jnp.float32)


def on_device(coefficients, hamiltonian, neighbours, pattern):
    elem_count = coefficients.shape[0]
    basis = coefficients.shape[1]
    local_states = coefficients.shape[2]
    elements = elem_count * lax.axis_size("elem")
    rows_total = elements * basis
    base_id = lax.axis_index("elem") * elem_count
    relative = jnp.mod(neighbours - base_id, elements)
    slots = jnp.where(relative >= elements - LAYER, relative - (elements - LAYER), relative + LAYER)
    weights = pattern[:, :, None, None].astype(jnp.bfloat16)
    start_block = coefficients.astype(jnp.float32)
    image_one = apply_hamiltonian(coefficients, hamiltonian, slots, weights)
    filtered_one = ((image_one - CENTER * start_block) / HALF_WIDTH).astype(jnp.bfloat16)
    image_two = apply_hamiltonian(filtered_one, hamiltonian, slots, weights)
    filtered_two = (
        2.0 * (image_two - CENTER * filtered_one.astype(jnp.float32)) / HALF_WIDTH - start_block
    ).astype(jnp.bfloat16)
    rows_local = filtered_two.reshape(elem_count * basis, local_states)
    contract = (((0,), (0,)), ((), ()))
    all_states = lax.all_gather(rows_local, "state", axis=1, tiled=True)
    partial_value = lax.dot_general(
        all_states, rows_local, contract, preferred_element_type=jnp.float32
    )
    offset = lax.axis_index("state") * local_states
    column_sum = lax.psum(partial_value, "elem")
    gram_matrix = lax.all_gather(column_sum, "state", axis=1, tiled=True)
    gram_matrix = gram_matrix / rows_total
    factor = jnp.linalg.cholesky(gram_matrix)
    row_ids = lax.broadcasted_iota(jnp.int32, (NS, local_states), 0)
    col_ids = lax.broadcasted_iota(jnp.int32, (NS, local_states), 1) + offset
    identity_cols = (row_ids == col_ids).astype(jnp.float32)
    rotation = lax.linalg.triangular_solve(
        factor, identity_cols, left_side=True, lower=True, transpose_a=True
    ).astype(jnp.bfloat16)
    new_rows = jnp.dot(all_states, rotation, preferred_element_type=jnp.float32).astype(
        jnp.bfloat16
    )
    return new_rows.reshape(elem_count, basis, local_states)


def solution(mesh):
    return jax.shard_map(
        on_device,
        mesh=mesh,
        in_specs=(
            P("elem", None, "state"),
            P("elem", None, None),
            P("elem", None),
            P("elem", None),
        ),
        out_specs=P("elem", None, "state"),
        check_vma=False,
    )
```

profile of v0, /device:TPU:1, one launch (start us, length us, event | category | flops | bytes accessed | tf_op | source)
XLA Modules:
  0.0 872.4 jit_solution(1561025889448329794)
XLA Ops:
  13.0 4.1 collective-permute-done
  21.3 13.3 %gather_fusion = bf16[384,64,128]{2,1,0:T(8,128)(2,1)} fusion(bf16[128,64,128]{2,1,0:T(8,128)(2,1)S(1)} %pad_maximum_fusion.2, s32[1024]{0:T(1024)S(1)} %pad_clamp_fusion), kind=kCustom, calls=%fused_computation | custom fusion | bytes 12584448 | tf_op jit(solution)/shard_map/gather | solution.py:32
  34.6 6.0 broadcast_multiply_fusion.1
  57.7 13.3 %gather_fusion.1 = bf16[384,64,128]{2,1,0:T(8,128)(2,1)} fusion(bf16[128,64,128]{2,1,0:T(8,128)(2,1)S(1)} %pad_maximum_fusion.3, s32[1024]{0:T(1024)S(1)} %pad_clamp_fusion), kind=kCustom, calls=%fused_computation.1 | custom fusion | bytes 12584448 | tf_op jit(solution)/shard_map/gather | solution.py:32
  71.0 6.0 broadcast_multiply_fusion
  80.5 5.1 fusion.4
  85.7 127.9 %all-gather.3.cloned.1.call-done = bf16[4096,1024]{1,0:T(8,128)(2,1)} async-done(((bf16[4096,128]{1,0:T(8,128)(2,1)}), bf16[4096,1024]{1,0:T(8,128)(2,1)}) %all-gather.3.cloned.1.call-update) | async-done | bytes 8388624 | tf_op jit(solution)/shard_map/all_gather | solution.py:57
  213.5 5.8 fusion.71
  219.4 221.7 %all-reduce.3.cloned.1.call-done = f32[1024,128]{0,1:T(8,128)} async-done(((f32[1024,128]{0,1:T(8,128)}), f32[1024,128]{0,1:T(8,128)}) %all-reduce.3.cloned.1.call-update) | async-done | bytes 524304 | tf_op jit(solution)/shard_map/psum | solution.py:62
  441.3 77.5 %all-gather.5.cloned.1.call-done = f32[1024,1024]{0,1:T(8,128)} async-done(((f32[1024,128]{0,1:T(8,128)}), f32[1024,1024]{0,1:T(8,128)}) %all-gather.5.cloned.1.call-update) | async-done | bytes 4194320 | tf_op jit(solution)/shard_map/all_gather | solution.py:63
  518.8 5.0 broadcast_multiply_fusion.2
  523.7 5.6 copy.15
  529.3 4.4 fusion
  535.7 11.7 %cholesky.223 = f32[128,128]{1,0:T(8,128)S(1)} custom-call(f32[128,128]{1,0:T(8,128)S(1)} %cholesky.580), custom_call_target="Cholesky" | custom-call | tf_op jit(solution)/shard_map/jit(cholesky)/cholesky | solution.py:65
  547.5 9.8 %custom-call.62 = f32[1,128,128]{1,2,0:T(8,128)S(1)} custom-call(f32[1,128,128]{2,1,0:T(8,128)S(1)} %get-tuple-element.48), custom_call_target="InvertDiagBlocksLowerTriangular" | custom-call | tf_op jit(solution)/shard_map/jit(cholesky)/cholesky | solution.py:65
  563.7 12.1 %cholesky.244 = f32[128,128]{1,0:T(8,128)S(1)} custom-call(f32[128,128]{1,0:T(8,128)S(1)} %cholesky.584), custom_call_target="Cholesky" | custom-call | tf_op jit(solution)/shard_map/jit(cholesky)/cholesky | solution.py:65
  576.5 9.8 %custom-call.63 = f32[1,128,128]{1,2,0:T(8,128)S(1)} custom-call(f32[1,128,128]{2,1,0:T(8,128)S(1)} %get-tuple-element.45), custom_call_target="InvertDiagBlocksLowerTriangular" | custom-call | tf_op jit(solution)/shard_map/jit(cholesky)/cholesky | solution.py:65
  589.6 11.7 %cholesky.468 = f32[128,128]{1,0:T(8,128)S(1)} custom-call(f32[128,128]{1,0:T(8,128)S(1)} %cholesky.589), custom_call_target="Cholesky" | custom-call | tf_op jit(solution)/shard_map/jit(cholesky)/cholesky | solution.py:65
  602.6 9.8 %custom-call.64 = f32[1,128,128]{1,2,0:T(8,128)S(1)} custom-call(f32[1,128,128]{2,1,0:T(8,128)S(1)} %get-tuple-element.42), custom_call_target="InvertDiagBlocksLowerTriangular" | custom-call | tf_op jit(solution)/shard_map/jit(cholesky)/cholesky | solution.py:65
  616.0 11.9 %cholesky.487 = f32[128,128]{1,0:T(8,128)S(1)} custom-call(f32[128,128]{1,0:T(8,128)S(1)} %cholesky.594), custom_call_target="Cholesky" | custom-call | tf_op jit(solution)/shard_map/jit(cholesky)/cholesky | solution.py:65
  629.2 9.8 %custom-call.65 = f32[1,128,128]{1,2,0:T(8,128)S(1)} custom-call(f32[1,128,128]{2,1,0:T(8,128)S(1)} %get-tuple-element.39), custom_call_target="InvertDiagBlocksLowerTriangular" | custom-call | tf_op jit(solution)/shard_map/jit(cholesky)/cholesky | solution.py:65
  642.5 11.7 %cholesky.506 = f32[128,128]{1,0:T(8,128)S(1)} custom-call(f32[128,128]{1,0:T(8,128)S(1)} %cholesky.599), custom_call_target="Cholesky" | custom-call | tf_op jit(solution)/shard_map/jit(cholesky)/cholesky | solution.py:65
  655.5 10.0 %custom-call.66 = f32[1,128,128]{1,2,0:T(8,128)S(1)} custom-call(f32[1,128,128]{2,1,0:T(8,128)S(1)} %get-tuple-element.36), custom_call_target="InvertDiagBlocksLowerTriangular" | custom-call | tf_op jit(solution)/shard_map/jit(cholesky)/cholesky | solution.py:65
  668.9 11.7 %cholesky.526 = f32[128,128]{1,0:T(8,128)S(1)} custom-call(f32[128,128]{1,0:T(8,128)S(1)} %cholesky.604), custom_call_target="Cholesky" | custom-call | tf_op jit(solution)/shard_map/jit(cholesky)/cholesky | solution.py:65
  681.9 9.8 %custom-call.67 = f32[1,128,128]{1,2,0:T(8,128)S(1)} custom-call(f32[1,128,128]{2,1,0:T(8,128)S(1)} %get-tuple-element.33), custom_call_target="InvertDiagBlocksLowerTriangular" | custom-call | tf_op jit(solution)/shard_map/jit(cholesky)/cholesky | solution.py:65
  694.7 12.1 %cholesky.546 = f32[128,128]{1,0:T(8,128)S(1)} custom-call(f32[128,128]{1,0:T(8,128)S(1)} %cholesky.609), custom_call_target="Cholesky" | custom-call | tf_op jit(solution)/shard_map/jit(cholesky)/cholesky | solution.py:65
  708.0 9.8 %custom-call.68 = f32[1,128,128]{1,2,0:T(8,128)S(1)} custom-call(f32[1,128,128]{2,1,0:T(8,128)S(1)} %get-tuple-element.30), custom_call_target="InvertDiagBlocksLowerTriangular" | custom-call | tf_op jit(solution)/shard_map/jit(cholesky)/cholesky | solution.py:65
  720.5 11.7 %cholesky.564 = f32[128,128]{1,0:T(8,128)S(1)} custom-call(f32[128,128]{1,0:T(8,128)S(1)} %convolution_subtract_fusion.11), custom_call_target="Cholesky" | custom-call | tf_op jit(solution)/shard_map/jit(cholesky)/cholesky | solution.py:65
  739.0 4.8 select_select_fusion
  743.8 23.6 %while.1 = (s32[]{:T(128)}, f32[1024,1024]{1,0:T(8,128)}, s32[8,2]{0,1:T(2,128)S(1)}, f32[8,128,128]{2,1,0:T(8,128)S(1)}, s32[]{:T(128)}) while((s32[]{:T(128)}, f32[1024,1024]{1,0:T(8,128)}, s32[8,2]{0,1:T(2,128)S(1)}, f32[8,128,128]{2,1,0:T(8,128)S(1)}, s32[]{:T(128)}) %tuple.42), condition=%wide.while_cond, body=%wide.while_body.sunk | while | flops 2 | bytes 131181 | solution.py:69
  767.4 78.8 %custom-call.69 = f32[8,128,128]{1,2,0:T(8,128)S(1)} custom-call(f32[8,128,128]{2,1,0:T(8,128)S(1)} %get-tuple-element.12), custom_call_target="InvertDiagBlocksLowerTriangular" | custom-call | tf_op jit(solution)/shard_map/triangular_solve | solution.py:69
  859.0 6.7 convolution_convert_fusion
  (137 shorter events, 104.1 us)
Async XLA Ops:
  6.5 207.0 %all-gather.3.cloned.1.call-start = ((), (), s32[]{:S(2)}) async-start(), calls=%async_computation | async-start | bytes 9437184 | tf_op jit(solution)/shard_map/all_gather | solution.py:57
  7.8 9.2 %collective-permute-start = (bf16[32,64,128]{2,1,0:T(8,128)(2,1)S(1)}, bf16[32,64,128]{2,1,0:T(8,128)(2,1)S(1)}, u32[]{:S(2)}, u32[]{:S(2)}) collective-permute-start(bf16[32,64,128]{2,1,0:T(8,128)(2,1)S(1)} %get-tuple-element.25), channel_id=1, source_target_pairs={{0,8},{8,16},{16,24},{24,32},{32,40},{40,48},{48,56},{56,64},{64,7... | collective-permute-start | bytes 1572872 | tf_op jit(solution)/shard_map/ppermute | solution.py:21
  10.9 8.9 %collective-permute-start.1 = (bf16[32,64,128]{2,1,0:T(8,128)(2,1)S(1)}, bf16[32,64,128]{2,1,0:T(8,128)(2,1)S(1)}, u32[]{:S(2)}, u32[]{:S(2)}) collective-permute-start(bf16[32,64,128]{2,1,0:T(8,128)(2,1)S(1)} %get-tuple-element.26), channel_id=1, source_target_pairs={{8,0},{16,8},{24,16},{32,24},{40,32},{48,40},{56,48},{64,56},{72,6... | collective-permute-start | bytes 1572872 | tf_op jit(solution)/shard_map/ppermute | solution.py:23
  34.6 6.0 copy-start
  48.1 9.3 %copy-start.1 = (bf16[64,64,128]{2,1,0:T(8,128)(2,1)}, bf16[64,64,128]{2,1,0:T(8,128)(2,1)S(1)}, u32[]{:S(2)}) copy-start(bf16[64,64,128]{2,1,0:T(8,128)(2,1)S(1)} %fusion.3) | copy-start | bytes 3145732
  48.2 6.2 collective-permute-start.2
  48.3 9.2 %collective-permute-start.3 = (bf16[32,64,128]{2,1,0:T(8,128)(2,1)S(1)}, bf16[32,64,128]{2,1,0:T(8,128)(2,1)S(1)}, u32[]{:S(2)}, u32[]{:S(2)}) collective-permute-start(bf16[32,64,128]{2,1,0:T(8,128)(2,1)S(1)} %get-tuple-element.24), channel_id=1, source_target_pairs={{8,0},{16,8},{24,16},{32,24},{40,32},{48,40},{56,48},{64,56},{72,6... | collective-permute-start | bytes 1572872 | tf_op jit(solution)/shard_map/ppermute | solution.py:23
  71.0 6.0 copy-start.2
  85.6 355.5 %all-reduce.3.cloned.1.call-start = ((), (), s32[]{:S(2)}) async-start(), calls=%async_computation.1 | async-start | bytes 1048576 | tf_op jit(solution)/shard_map/psum | solution.py:62
  219.3 299.4 %all-gather.5.cloned.1.call-start = ((), (), s32[]{:S(2)}) async-start(), calls=%async_computation.2 | async-start | bytes 4718592 | tf_op jit(solution)/shard_map/all_gather | solution.py:63
  533.7 2.0 copy-start.3
Sparse Core Ops, SparseCore 0:
  85.7 127.7 all-gather.2
  219.5 221.5 all-reduce.2
  444.1 74.6 all-gather.4
where the time goes:
time: 882 us; the launch traced here: 872 us
  waiting for transfers between devices  440 us (50%)
  other arithmetic  288 us (33%)
  local copies, waits for them, and re-layouts  62 us (7%)
  matrix products  57.1 us (6%)
  between operations  18.8 us (2%)
    psum x1, waiting for transfers between devices, on_device(): column_sum = lax.psum(partial_value, 'elem')  222 us
    another operation x30, other arithmetic, on_device(): factor = jnp.linalg.cholesky(gram_matrix)  173 us
    all_gather x1, waiting for transfers between devices, on_device(): all_states = lax.all_gather(rows_local, 'state', axis=1, tiled=True)  128 us
    another operation x4, other arithmetic, on_device(): lax.linalg.triangular_solve(factor, identity_cols, left_side=True, lower=...  83.6 us
    all_gather x1, waiting for transfers between devices, on_device(): gram_matrix = lax.all_gather(column_sum, 'state', axis=1, tiled=True)  77.5 us
    gather x2, local copies, waits for them, and re-layouts, apply_hamiltonian(): gathered = padded[slots] * weights  26.7 us
    another operation x24, local copies, waits for them, and re-layouts  23.4 us
    another operation x14, matrix products, on_device(): factor = jnp.linalg.cholesky(gram_matrix)  23.1 us
  transfers between devices with their start and end apart: 7, of which 7 were waited for; matrix products, arithmetic and copies ran while one was open for 0% of the time, Pallas kernels for 0%

commit v1 on v0

v1 whole, which is shorter than its diff:
```python
import functools

import jax
import jax.numpy as jnp
from jax import lax
from jax.experimental import pallas as pl
from jax.experimental.pallas import tpu as pltpu
from jax.sharding import PartitionSpec as P

LAYER = 32
CENTER = 0.5
HALF_WIDTH = 2.0
BLK = 128
BASE = 32
F32 = jnp.float32
BF16 = jnp.bfloat16
HIGHEST = lax.Precision.HIGHEST
MESH = pl.DeviceIdType.MESH
VMEM = pltpu.VMEM
MIB = 1024 * 1024


def in_vmem():
    return pl.BlockSpec(memory_space=pltpu.VMEM)


def in_smem():
    return pl.BlockSpec(memory_space=pltpu.SMEM)


def greet(devices):
    barrier = pltpu.get_barrier_semaphore()
    for device in devices:
        pl.semaphore_signal(barrier, inc=1, device_id=device, device_id_type=MESH)
    pl.semaphore_wait(barrier, len(devices))


def remote(src, dst, send, recv, device):
    return pltpu.make_async_remote_copy(
        src_ref=src, dst_ref=dst, send_sem=send, recv_sem=recv, device_id=device, device_id_type=MESH
    )


def filter_kernel(
    elems, states, nbr, pat, v_ref, h_ref, z_ref, g_ref,
    acc, f_ref, y_ref, tail_a, head_a, tail_b, head_b, halo_send, halo_recv, swap_send, swap_recv,
):
    count, basis, width = v_ref.shape
    rows = count * basis // states
    per = count // states
    me = lax.axis_index("elem")
    ms = lax.axis_index("state")
    right = lax.rem(me + 1, elems)
    left = lax.rem(me + elems - 1, elems)
    peers = [lax.rem(ms + d, states) for d in range(states)]
    greet([{"elem": right}, {"elem": left}] + [{"state": peers[d]} for d in range(1, states)])

    halo = ((tail_a, head_a), (tail_b, head_b))

    def exchange(stage, src):
        tail = remote(
            src.at[pl.ds(count - LAYER, LAYER)], halo[stage][0],
            halo_send.at[stage, 0], halo_recv.at[stage, 0], {"elem": right},
        )
        head = remote(
            src.at[pl.ds(0, LAYER)], halo[stage][1],
            halo_send.at[stage, 1], halo_recv.at[stage, 1], {"elem": left},
        )
        return tail, head

    def local_part(src):
        def body(e, carry):
            parts = [src[e]]
            for f in range(6):
                n = nbr[e, f]
                w = (pat[e, f] * (n // count == me).astype(jnp.int32)).astype(F32)
                parts.append(src[lax.rem(n, count)] * jnp.full((basis, width), w, F32).astype(BF16))
            stacked = jnp.concatenate(parts, axis=0)
            acc[e] = jnp.dot(h_ref[e], stacked, preferred_element_type=F32)
            return carry

        lax.fori_loop(0, count, body, 0, unroll=4)

    def image(stage, e, layer):
        face = 0 if layer == 1 else 1
        side = 1 if layer == 1 else 0
        w = pat[e, face].astype(F32)
        block = halo[stage][side][lax.rem(nbr[e, face], LAYER)]
        block = block * jnp.full((basis, width), w, F32).astype(BF16)
        strip = h_ref[e, :, (1 + face) * basis:(2 + face) * basis]
        return acc[e] + jnp.dot(strip, block, preferred_element_type=F32)

    first = exchange(0, v_ref)
    for c in first:
        c.start()
    local_part(v_ref)
    second = exchange(1, f_ref)
    for layer in range(2):
        first[layer].wait_recv()

        def one(i, carry):
            e = layer * LAYER + i
            f_ref[e] = ((image(0, e, layer) - CENTER * v_ref[e].astype(F32)) / HALF_WIDTH).astype(BF16)
            return carry

        lax.fori_loop(0, LAYER, one, 0, unroll=4)
        second[1 - layer].start()
    local_part(f_ref)
    swaps = [None] + [
        remote(
            y_ref.at[pl.ds(peers[d] * rows, rows)], z_ref.at[:, pl.ds(ms * width, width)],
            swap_send.at[d], swap_recv.at[d], {"state": peers[d]},
        )
        for d in range(1, states)
    ]
    for layer in range(2):
        second[layer].wait_recv()

        def two(i, carry):
            e = layer * LAYER + i
            out = 2.0 * (image(1, e, layer) - CENTER * f_ref[e].astype(F32)) / HALF_WIDTH
            y_ref[pl.ds(pl.multiple_of(e * basis, basis), basis), :] = (out - v_ref[e].astype(F32)).astype(BF16)
            return carry

        lax.fori_loop(0, LAYER, two, 0, unroll=4)
    for d in range(1, states):
        swaps[d].start()
    z_ref[:, pl.ds(pl.multiple_of(ms * width, width), width)] = y_ref[
        pl.ds(pl.multiple_of(ms * rows, rows), rows), :
    ]
    for c in first + second:
        c.wait_send()
    for d in range(1, states):
        swaps[d].wait()

    blocks = states * width // BLK
    offset = 0
    for k in range(blocks):
        strip = lax.dot_general(
            z_ref[:, k * BLK:(k + 1) * BLK], z_ref[:, k * BLK:], (((0,), (0,)), ((), ())),
            preferred_element_type=F32,
        )
        for j in range(blocks - k):
            g_ref[offset * BLK:(offset + 1) * BLK, :] = strip[:, j * BLK:(j + 1) * BLK]
            offset += 1


def filter_and_gram(coefficients, hamiltonian, neighbours, pattern, elems, states):
    count, basis, width = coefficients.shape
    rows = count * basis // states
    blocks = states * width // BLK
    packed = blocks * (blocks + 1) // 2 * BLK
    return pl.pallas_call(
        functools.partial(filter_kernel, elems, states),
        out_shape=(
            jax.ShapeDtypeStruct((rows, states * width), BF16),
            jax.ShapeDtypeStruct((packed, BLK), F32),
        ),
        in_specs=[in_smem(), in_smem(), in_vmem(), in_vmem()],
        out_specs=(in_vmem(), in_vmem()),
        scratch_shapes=[
            VMEM((count, basis, width), F32),
            VMEM((count, basis, width), BF16),
            VMEM((count * basis, width), BF16),
            VMEM((LAYER, basis, width), BF16),
            VMEM((LAYER, basis, width), BF16),
            VMEM((LAYER, basis, width), BF16),
            VMEM((LAYER, basis, width), BF16),
            pltpu.SemaphoreType.DMA((2, 2)),
            pltpu.SemaphoreType.DMA((2, 2)),
            pltpu.SemaphoreType.DMA((states,)),
            pltpu.SemaphoreType.DMA((states,)),
        ],
        compiler_params=pltpu.CompilerParams(
            collective_id=0, has_side_effects=True, vmem_limit_bytes=40 * MIB
        ),
        cost_estimate=pl.CostEstimate(flops=2 * 10**9, bytes_accessed=8 * MIB, transcendentals=0),
    )(neighbours, pattern, coefficients, hamiltonian)


SIZES = (4, 4, 8)


def sum_kernel(
    src, res, pair, acc, buf_a, buf_b, buf_c, core_send, core_recv, up_send, up_recv, down_send, down_recv,
):
    total = src.shape[0]
    half = total // 2
    part = half // 3
    me = lax.axis_index("elem")
    ms = lax.axis_index("state")
    core = lax.rem(me, 2)
    place = [lax.rem(ms, 4), (ms // 4) * 2 + me // 16, lax.rem(me, 16) // 2]

    def device(dim, at, c):
        spot = list(place)
        if dim is not None:
            spot[dim] = at
        x, y, z = spot
        return {"elem": lax.rem(y, 2) * 16 + z * 2 + c, "state": (y // 2) * 4 + x}

    def peer(dim, d):
        return lax.rem(place[dim] + d, SIZES[dim])

    other = device(None, None, 1 - core)
    greet([other] + [device(dim, peer(dim, d), core) for dim in range(3) for d in range(1, SIZES[dim])])

    mine = pl.multiple_of(core * half, 8)
    theirs = pl.multiple_of((1 - core) * half, 8)
    swap = remote(src.at[pl.ds(theirs, half)], pair, core_send.at[3], core_recv.at[3], other)
    swap.start()
    swap.wait()
    acc[...] = src[pl.ds(mine, half), :] + pair[...]

    orders = [[p % 3, (p + 1) % 3, (p + 2) % 3] for p in range(3)]
    len_a = [part // SIZES[o[0]] for o in orders]
    len_b = [len_a[p] // SIZES[orders[p][1]] for p in range(3)]
    base_a = [p * part + place[orders[p][0]] * len_a[p] for p in range(3)]
    base_b = [base_a[p] + place[orders[p][1]] * len_b[p] for p in range(3)]

    for level, buf in ((0, buf_a), (1, buf_b)):
        copies = [[] for _ in range(3)]
        for p in range(3):
            dim = orders[p][level]
            length = (len_a, len_b)[level][p]
            start = p * part if level == 0 else base_a[p]
            for d in range(1, SIZES[dim]):
                to = peer(dim, d)
                copies[p].append(
                    remote(
                        acc.at[pl.ds(pl.multiple_of(start + to * length, 8), length)],
                        buf.at[p, d, pl.ds(0, length)],
                        up_send.at[level, p, d], up_recv.at[level, p, d], device(dim, to, core),
                    )
                )
        for d in range(7):
            for p in range(3):
                if d < len(copies[p]):
                    copies[p][d].start()
        for p in range(3):
            dim = orders[p][level]
            length = (len_a, len_b)[level][p]
            start = p * part if level == 0 else base_a[p]
            own = pl.ds(pl.multiple_of(start + place[dim] * length, 8), length)
            total_rows = acc[own, :]
            for d in range(1, SIZES[dim]):
                copies[p][d - 1].wait_recv()
                total_rows = total_rows + buf[p, d, pl.ds(0, length), :]
            acc[own, :] = total_rows
        for p in range(3):
            for c in copies[p]:
                c.wait_send()

    copies = [[] for _ in range(3)]
    for p in range(3):
        dim = orders[p][2]
        length = len_b[p]
        spot = pl.ds(pl.multiple_of(base_b[p], 8), length)
        for d in range(1, SIZES[dim]):
            copies[p].append(
                remote(
                    acc.at[spot], buf_c.at[p, place[dim], pl.ds(0, length)],
                    up_send.at[2, p, d], up_recv.at[2, p, d], device(dim, peer(dim, d), core),
                )
            )
        buf_c[p, pl.ds(place[dim], 1), pl.ds(0, length), :] = acc[spot, :][None]
    for d in range(7):
        for p in range(3):
            if d < len(copies[p]):
                copies[p][d].start()
    for p in range(3):
        dim = orders[p][2]
        length = len_b[p]
        for c in copies[p]:
            c.wait_recv()
        total_rows = buf_c[p, 0, pl.ds(0, length), :]
        for i in range(1, SIZES[dim]):
            total_rows = total_rows + buf_c[p, i, pl.ds(0, length), :]
        res[pl.ds(pl.multiple_of(mine + base_b[p], 8), length), :] = total_rows
    for p in range(3):
        for c in copies[p]:
            c.wait_send()

    for level in (1, 0):
        copies = [[] for _ in range(3)]
        for p in range(3):
            dim = orders[p][level]
            length = (len_a, len_b)[level][p]
            start = (base_a, base_b)[level][p]
            spot = pl.ds(pl.multiple_of(mine + start, 8), length)
            for d in range(1, SIZES[dim]):
                copies[p].append(
                    remote(
                        res.at[spot], res.at[spot],
                        down_send.at[level, p, d], down_recv.at[level, p, d], device(dim, peer(dim, d), core),
                    )
                )
        for d in range(7):
            for p in range(3):
                if d < len(copies[p]):
                    copies[p][d].start()
        for p in range(3):
            for c in copies[p]:
                c.wait()
    last = []
    for p in range(3):
        spot = pl.ds(pl.multiple_of(mine + p * part, 8), part)
        last.append(remote(res.at[spot], res.at[spot], core_send.at[p], core_recv.at[p], other))
        last[p].start()
    for c in last:
        c.wait()


def sum_everywhere(packed):
    total = packed.shape[0]
    part = total // 6
    return pl.pallas_call(
        sum_kernel,
        out_shape=jax.ShapeDtypeStruct(packed.shape, F32),
        in_specs=[in_vmem()],
        out_specs=in_vmem(),
        scratch_shapes=[
            VMEM((total // 2, BLK), F32),
            VMEM((total // 2, BLK), F32),
            VMEM((3, 8, part // 4, BLK), F32),
            VMEM((3, 8, part // 16, BLK), F32),
            VMEM((3, 8, part // 16, BLK), F32),
            pltpu.SemaphoreType.DMA((4,)),
            pltpu.SemaphoreType.DMA((4,)),
            pltpu.SemaphoreType.DMA((3, 3, 8)),
            pltpu.SemaphoreType.DMA((3, 3, 8)),
            pltpu.SemaphoreType.DMA((2, 3, 8)),
            pltpu.SemaphoreType.DMA((2, 3, 8)),
        ],
        compiler_params=pltpu.CompilerParams(
            collective_id=1, has_side_effects=True, vmem_limit_bytes=40 * MIB
        ),
        cost_estimate=pl.CostEstimate(flops=10**7, bytes_accessed=5 * MIB, transcendentals=0),
    )(packed)


def tdot(a, b):
    return lax.dot_general(a, b, (((0,), (0,)), ((), ())), precision=HIGHEST, preferred_element_type=F32)


def base_step(p, tile):
    r0 = pl.multiple_of(p * BASE, BASE)
    panel = tile[pl.ds(r0, BASE), :]
    rolled = pltpu.roll(panel, lax.rem(BLK - r0, BLK), 1)
    lane = lax.broadcasted_iota(jnp.int32, (8, BLK), 1)
    sub = lax.broadcasted_iota(jnp.int32, (8, BLK), 0)
    groups = BASE // 8
    cols = [
        [jnp.broadcast_to(rolled[8 * g:8 * g + 8, k:k + 1], (8, BLK)) for g in range(groups)]
        for k in range(BASE)
    ]
    inside = (lane >= r0) & (lane < r0 + BASE)
    rows = [
        jnp.where(inside, (lane - r0 == sub + 8 * g).astype(F32), panel[8 * g:8 * g + 8])
        for g in range(groups)
    ]
    scales = [jnp.zeros((8, BLK), F32) for _ in range(groups)]
    for j in range(BASE):
        gj, sj = divmod(j, 8)
        pivot = jnp.broadcast_to(cols[j][gj][sj:sj + 1], (8, BLK))
        inverse = 1.0 / pivot
        scales[gj] = jnp.where(sub == sj, pivot, scales[gj])
        ratio = [None] * groups
        for g in range(gj, groups):
            ratio[g] = cols[j][g] * inverse
            if g == gj:
                ratio[g] = jnp.where(sub > sj, ratio[g], 0.0)
        for k in range(j + 1, BASE):
            row = jnp.broadcast_to(cols[k][gj][sj:sj + 1], (8, BLK))
            for g in range(gj, groups):
                if 8 * g + 7 > j:
                    cols[k][g] = cols[k][g] - ratio[g] * row
        row = jnp.broadcast_to(rows[gj][sj:sj + 1], (8, BLK))
        for g in range(gj, groups):
            if 8 * g + 7 > j:
                rows[g] = rows[g] - ratio[g] * row
    done = jnp.concatenate([rows[g] * lax.rsqrt(scales[g]) for g in range(groups)], axis=0)
    wide = lax.broadcasted_iota(jnp.int32, (BASE, BLK), 1)
    below = jnp.where(wide >= r0 + BASE, done, 0.0)
    update = tdot(below, done)
    rr = lax.broadcasted_iota(jnp.int32, (BLK, BLK), 0)
    cc = lax.broadcasted_iota(jnp.int32, (BLK, BLK), 1)
    clear = (rr >= r0 + BASE) & (cc >= r0) & (cc < r0 + BASE)
    tile[...] = jnp.where(clear, 0.0, tile[...]) - update
    tile[pl.ds(r0, BASE), :] = done


def inverse_kernel(n, scale, g_ref, x_ref, mat, tile):
    blocks = n // BLK
    offset = 0
    for k in range(blocks):
        for j in range(k, blocks):
            mat[k * BLK:(k + 1) * BLK, j * BLK:(j + 1) * BLK] = (
                g_ref[offset * BLK:(offset + 1) * BLK, :] * scale
            )
            offset += 1
    rr = lax.broadcasted_iota(jnp.int32, (BLK, BLK), 0)
    cc = lax.broadcasted_iota(jnp.int32, (BLK, BLK), 1)

    def step(k, carry):
        rows = pl.ds(pl.multiple_of(k * BLK, BLK), BLK)
        tile[...] = mat[rows, rows]

        def inner(p, c):
            base_step(p, tile)
            return c

        lax.fori_loop(0, BLK // BASE, inner, 0)
        corner = jnp.where(cc <= rr, tile[...], 0.0)
        mat[rows, rows] = (rr == cc).astype(F32)
        mat[rows, :] = jnp.dot(corner, mat[rows, :], precision=HIGHEST, preferred_element_type=F32)

        def update(i, c):
            at = pl.ds(pl.multiple_of(i * BLK, BLK), BLK)
            left = mat[rows, at]
            mat[at, rows] = jnp.zeros((BLK, BLK), F32)
            mat[at, :] = mat[at, :] - tdot(left, mat[rows, :])
            return c

        lax.fori_loop(k + 1, blocks, update, 0)
        return carry

    lax.fori_loop(0, blocks, step, 0)
    for k in range(blocks):
        for j in range(blocks):
            spot = (slice(k * BLK, (k + 1) * BLK), slice(j * BLK, (j + 1) * BLK))
            if j > k:
                x_ref[spot] = jnp.zeros((BLK, BLK), x_ref.dtype)
            elif j < k:
                x_ref[spot] = mat[spot].astype(x_ref.dtype)
            else:
                x_ref[spot] = jnp.where(cc <= rr, mat[spot], 0.0).astype(x_ref.dtype)


def inverse_factor(packed, n, scale):
    return pl.pallas_call(
        functools.partial(inverse_kernel, n, scale),
        out_shape=jax.ShapeDtypeStruct((n, n), BF16),
        in_specs=[in_vmem()],
        out_specs=in_vmem(),
        scratch_shapes=[VMEM((n, n), F32), VMEM((BLK, BLK), F32)],
        compiler_params=pltpu.CompilerParams(vmem_limit_bytes=40 * MIB),
        cost_estimate=pl.CostEstimate(flops=6 * n**3, bytes_accessed=4 * n * n, transcendentals=0),
    )(packed)


def rotate_kernel(states, z_ref, x_ref, o_ref, out, send, recv):
    rows, n = z_ref.shape
    width = n // states
    ms = lax.axis_index("state")
    peers = [lax.rem(ms + d, states) for d in range(states)]
    greet([{"state": peers[d]} for d in range(1, states)])
    mine = pl.ds(pl.multiple_of(ms * rows, rows), rows)
    copies = []
    for d in list(range(1, states)) + [0]:
        at = pl.ds(pl.multiple_of(peers[d] * width, width), width)
        block = lax.dot_general(
            z_ref[...], x_ref[at, :], (((1,), (1,)), ((), ())), preferred_element_type=F32
        ).astype(BF16)
        if d == 0:
            o_ref[mine, :] = block
        else:
            out[d] = block
            copies.append(remote(out.at[d], o_ref.at[mine], send.at[d], recv.at[d], {"state": peers[d]}))
            copies[-1].start()
    for c in copies:
        c.wait()


def rotate(rows, inverse, states):
    count, n = rows.shape
    width = n // states
    return pl.pallas_call(
        functools.partial(rotate_kernel, states),
        out_shape=jax.ShapeDtypeStruct((count * states, width), BF16),
        in_specs=[in_vmem(), in_vmem()],
        out_specs=in_vmem(),
        scratch_shapes=[
            VMEM((states, count, width), BF16),
            pltpu.SemaphoreType.DMA((states,)),
            pltpu.SemaphoreType.DMA((states,)),
        ],
        compiler_params=pltpu.CompilerParams(
            collective_id=2, has_side_effects=True, vmem_limit_bytes=40 * MIB
        ),
        cost_estimate=pl.CostEstimate(flops=2 * count * n * n, bytes_accessed=4 * MIB, transcendentals=0),
    )(rows, inverse)


def on_device(coefficients, hamiltonian, neighbours, pattern):
    count, basis, width = coefficients.shape
    elems = lax.axis_size("elem")
    states = lax.axis_size("state")
    rows, gram = filter_and_gram(coefficients, hamiltonian, neighbours, pattern, elems, states)
    gram = sum_everywhere(gram)
    inverse = inverse_factor(gram, states * width, 1.0 / (count * elems * basis))
    result = rotate(rows, inverse, states)
    return result.reshape(count, basis, width)


def solution(mesh):
    return jax.shard_map(
        on_device,
        mesh=mesh,
        in_specs=(
            P("elem", None, "state"),
            P("elem", None, None),
            P("elem", None),
            P("elem", None),
        ),
        out_specs=P("elem", None, "state"),
        check_vma=False,
    )
```

time: 882 us -> 184 us (0.21); the launches traced: 872 us -> 183 us
  waiting for transfers between devices: 440 us -> 0 us
  other arithmetic: 288 us -> 0 us
  Pallas kernels: 0 us -> 178 us
  matrix products: 57.1 us -> 0 us
  local copies, waits for them, and re-layouts: 62 us -> 5.93 us
  between operations: 18.8 us -> 0.04 us
    another operation x34 -> x0, other arithmetic: 256 us -> none  [the longest x30 173 us: on_device(): factor = jnp.linalg.cholesky(gram_matrix)]
    psum x1 -> x0, waiting for transfers between devices: 222 us -> none  [on_device(): column_sum = lax.psum(partial_value, 'elem')]
    all_gather x2 -> x0, waiting for transfers between devices: 205 us -> none  [the longest x1 128 us: on_device(): all_states = lax.all_gather(rows_local, 'state', axis=1, tiled=True)]
    pallas_call x0 -> x4, Pallas kernels: none -> 178 us  [the longest x1 59.4 us: sum_everywhere(): pl.pallas_call(sum_kernel, out_shape=jax.ShapeDtypeStruct(packed.shape, F...]
    another operation x29 -> x0, matrix products: 35.5 us -> none  [the longest x14 23.1 us: on_device(): factor = jnp.linalg.cholesky(gram_matrix)]
    gather x2 -> x0, local copies, waits for them, and re-layouts: 26.7 us -> none  [apply_hamiltonian(): gathered = padded[slots] * weights]
    another operation x36 -> x0, local copies, waits for them, and re-layouts: 26 us -> none
    dot_general x4 -> x0, matrix products: 21.6 us -> none  [the longest x2 9.12 us: apply_hamiltonian(): jnp.einsum('eik,eks->eis', hamilton, stacked, preferred_element_type=jnp....]
  transfers between devices with their start and end apart: 7 -> 0, of which waited for: 7 -> 0; matrix products, arithmetic and copies ran while one was open for 0% -> 0% of each run, Pallas kernels for 0% -> 0%
where the time goes in v1:
time: 184 us; the launch traced here: 183 us
  Pallas kernels  178 us (97%)
  local copies, waits for them, and re-layouts  5.93 us (3%)
    pallas_call x1, Pallas kernels, sum_everywhere(): pl.pallas_call(sum_kernel, out_shape=jax.ShapeDtypeStruct(packed.shape, F...  59.4 us
    pallas_call x1, Pallas kernels, inverse_factor(): pl.pallas_call(functools.partial(inverse_kernel, n, scale), out_shape=jax...  59.3 us
    pallas_call x1, Pallas kernels, filter_and_gram(): pl.pallas_call(functools.partial(filter_kernel, elems, states), out_shape...  38.6 us
    pallas_call x1, Pallas kernels, rotate(): pl.pallas_call(functools.partial(rotate_kernel, states), out_shape=jax.Sh...  20.3 us
    unnamed x7, local copies, waits for them, and re-layouts  5.93 us

profile of v1, /device:TPU:1, one launch (start us, length us, event | category | flops | bytes accessed | tf_op | source)
XLA Modules:
  0.0 183.5 jit_solution(15992071759928611495)
XLA Ops:
  0.0 0.8 copy.5.nbr
  0.8 0.8 copy.6.pat
  1.6 0.0 copy-start
  1.6 2.2 %copy-done = bf16[64,64,448]{2,1,0:T(8,128)(2,1)S(1)} copy-done((bf16[64,64,448]{2,1,0:T(8,128)(2,1)S(1)}, bf16[64,64,448]{2,1,0:T(8,128)(2,1)}, u32[]{:S(2)}) %copy-start) | copy-done | bytes 3670040
  3.7 0.0 copy-start.1
  3.7 1.2 copy-done.1
  5.0 38.6 %shard_map.46 = (bf16[512,1024]{1,0:T(8,128)(2,1)S(1)}, f32[4608,128]{1,0:T(8,128)S(1)}) custom-call(s32[64,6]{1,0:T(8,128)S(1)} %copy.5.nbr, s32[64,6]{1,0:T(8,128)S(1)} %copy.6.pat, bf16[64,64,128]{2,1,0:T(8,128)(2,1)S(1)} %copy-done.1, bf16[64,64,448]{2,1,0:T(8,128)(2,1)S(1)} %copy-done), custom_call_target="tpu_custom_call" | custom-call | flops 2000000000 | bytes 8388608 | tf_op jit(solution)/shard_map/pallas_call | solution.py:153
  43.6 59.4 %shard_map.47.g_ref = f32[4608,128]{1,0:T(8,128)S(1)} custom-call(f32[4608,128]{1,0:T(8,128)S(1)} %get-tuple-element.8.src), custom_call_target="tpu_custom_call" | custom-call | flops 10000000 | bytes 5242880 | tf_op jit(solution)/shard_map/pallas_call | solution.py:317
  103.0 59.3 %shard_map.48.x_ref = bf16[1024,1024]{1,0:T(8,128)(2,1)S(1)} custom-call(f32[4608,128]{1,0:T(8,128)S(1)} %shard_map.47.g_ref), custom_call_target="tpu_custom_call" | custom-call | flops 6442450944 | bytes 4194304 | tf_op jit(solution)/shard_map/pallas_call | solution.py:441
  162.2 20.3 %shard_map.49 = bf16[4096,128]{1,0:T(8,128)(2,1)S(1)} custom-call(bf16[512,1024]{1,0:T(8,128)(2,1)S(1)} %get-tuple-element.7.z_ref, bf16[1024,1024]{1,0:T(8,128)(2,1)S(1)} %shard_map.48.x_ref), custom_call_target="tpu_custom_call" | custom-call | flops 1073741824 | bytes 4194304 | tf_op jit(solution)/shard_map/pallas_call | solution.py:478
  182.5 1.0 copy.8
Async XLA Ops:
  1.6 2.2 %copy-start = (bf16[64,64,448]{2,1,0:T(8,128)(2,1)S(1)}, bf16[64,64,448]{2,1,0:T(8,128)(2,1)}, u32[]{:S(2)}) copy-start(bf16[64,64,448]{2,1,0:T(8,128)(2,1)} %h_ref.1) | copy-start | bytes 11010052
  3.7 1.2 copy-start.1

commit v2 on v1

--- a/solution.py
+++ b/solution.py
@@ -14,7 +14,6 @@
 BASE = 32
 F32 = jnp.float32
 BF16 = jnp.bfloat16
-HIGHEST = lax.Precision.HIGHEST
 MESH = pl.DeviceIdType.MESH
 VMEM = pltpu.VMEM
 MIB = 1024 * 1024
@@ -22,6 +21,10 @@
 
 def in_vmem():
     return pl.BlockSpec(memory_space=pltpu.VMEM)
+
+
+def in_hbm():
+    return pl.BlockSpec(memory_space=pl.ANY)
 
 
 def in_smem():
@@ -42,8 +45,8 @@
 
 
 def filter_kernel(
-    elems, states, nbr, pat, v_ref, h_ref, z_ref, g_ref,
-    acc, f_ref, y_ref, tail_a, head_a, tail_b, head_b, halo_send, halo_recv, swap_send, swap_recv,
+    elems, states, nbr, pat, v_hbm, h_hbm, z_ref, g_ref,
+    v_ref, h_ref, load, acc, f_ref, y_ref, tail_a, head_a, tail_b, head_b, halo_send, halo_recv, swap_send, swap_recv,
 ):
     count, basis, width = v_ref.shape
     rows = count * basis // states
@@ -53,6 +56,10 @@
     right = lax.rem(me + 1, elems)
     left = lax.rem(me + elems - 1, elems)
     peers = [lax.rem(ms + d, states) for d in range(states)]
+    load_v = pltpu.make_async_copy(v_hbm, v_ref, load.at[0])
+    load_h = pltpu.make_async_copy(h_hbm, h_ref, load.at[1])
+    load_v.start()
+    load_h.start()
     greet([{"elem": right}, {"elem": left}] + [{"state": peers[d]} for d in range(1, states)])
 
     halo = ((tail_a, head_a), (tail_b, head_b))
@@ -72,8 +79,8 @@
         def body(e, carry):
             parts = [src[e]]
             for f in range(6):
-                n = nbr[e, f]
-                w = (pat[e, f] * (n // count == me).astype(jnp.int32)).astype(F32)
+                n = nbr[f, e]
+                w = (pat[f, e] * (n // count == me).astype(jnp.int32)).astype(F32)
                 parts.append(src[lax.rem(n, count)] * jnp.full((basis, width), w, F32).astype(BF16))
             stacked = jnp.concatenate(parts, axis=0)
             acc[e] = jnp.dot(h_ref[e], stacked, preferred_element_type=F32)
@@ -84,15 +91,17 @@
     def image(stage, e, layer):
         face = 0 if layer == 1 else 1
         side = 1 if layer == 1 else 0
-        w = pat[e, face].astype(F32)
-        block = halo[stage][side][lax.rem(nbr[e, face], LAYER)]
+        w = pat[face, e].astype(F32)
+        block = halo[stage][side][lax.rem(nbr[face, e], LAYER)]
         block = block * jnp.full((basis, width), w, F32).astype(BF16)
         strip = h_ref[e, :, (1 + face) * basis:(2 + face) * basis]
         return acc[e] + jnp.dot(strip, block, preferred_element_type=F32)
 
+    load_v.wait()
     first = exchange(0, v_ref)
     for c in first:
         c.start()
+    load_h.wait()
     local_part(v_ref)
     second = exchange(1, f_ref)
     for layer in range(2):
@@ -156,9 +165,12 @@
             jax.ShapeDtypeStruct((rows, states * width), BF16),
             jax.ShapeDtypeStruct((packed, BLK), F32),
         ),
-        in_specs=[in_smem(), in_smem(), in_vmem(), in_vmem()],
+        in_specs=[in_smem(), in_smem(), in_hbm(), in_hbm()],
         out_specs=(in_vmem(), in_vmem()),
         scratch_shapes=[
+            VMEM(coefficients.shape, BF16),
+            VMEM(hamiltonian.shape, BF16),
+            pltpu.SemaphoreType.DMA((2,)),
             VMEM((count, basis, width), F32),
             VMEM((count, basis, width), BF16),
             VMEM((count * basis, width), BF16),
@@ -175,7 +187,7 @@
             collective_id=0, has_side_effects=True, vmem_limit_bytes=40 * MIB
         ),
         cost_estimate=pl.CostEstimate(flops=2 * 10**9, bytes_accessed=8 * MIB, transcendentals=0),
-    )(neighbours, pattern, coefficients, hamiltonian)
+    )(neighbours.T, pattern.T, coefficients, hamiltonian)
 
 
 SIZES = (4, 4, 8)
@@ -339,157 +351,208 @@
     )(packed)
 
 
-def tdot(a, b):
-    return lax.dot_general(a, b, (((0,), (0,)), ((), ())), precision=HIGHEST, preferred_element_type=F32)
-
-
-def base_step(p, tile):
-    r0 = pl.multiple_of(p * BASE, BASE)
-    panel = tile[pl.ds(r0, BASE), :]
-    rolled = pltpu.roll(panel, lax.rem(BLK - r0, BLK), 1)
+def recip(x):
+    q = pl.reciprocal(x, approx=True)
+    return q * (2.0 - x * q)
+
+
+def split(x):
+    h = x.astype(BF16)
+    r = x - h.astype(F32)
+    m = r.astype(BF16)
+    return h, m, (r - m.astype(F32)).astype(BF16)
+
+
+def left_stack(x):
+    h, m, l = split(x)
+    return jnp.concatenate([h, h, m, h, m, l], axis=0)
+
+
+def right_stack(x):
+    h, m, l = split(x)
+    return jnp.concatenate([h, m, h, l, m, h], axis=0)
+
+
+def sdot(a, b):
+    return lax.dot_general(a, b, (((0,), (0,)), ((), ())), preferred_element_type=F32)
+
+
+def base_step(p, panel):
+    r0 = p * BASE
     lane = lax.broadcasted_iota(jnp.int32, (8, BLK), 1)
     sub = lax.broadcasted_iota(jnp.int32, (8, BLK), 0)
     groups = BASE // 8
+    rows = [panel[8 * g:8 * g + 8] for g in range(groups)]
     cols = [
-        [jnp.broadcast_to(rolled[8 * g:8 * g + 8, k:k + 1], (8, BLK)) for g in range(groups)]
+        {g: jnp.broadcast_to(rows[g][:, r0 + k:r0 + k + 1], (8, BLK)) for g in range(k // 8, groups)}
         for k in range(BASE)
     ]
     inside = (lane >= r0) & (lane < r0 + BASE)
     rows = [
-        jnp.where(inside, (lane - r0 == sub + 8 * g).astype(F32), panel[8 * g:8 * g + 8])
-        for g in range(groups)
+        jnp.where(inside, (lane - r0 == sub + 8 * g).astype(F32), rows[g]) for g in range(groups)
     ]
-    scales = [jnp.zeros((8, BLK), F32) for _ in range(groups)]
-    for j in range(BASE):
+    scales = [jnp.ones((8, BLK), F32) for _ in range(groups)]
+
+    def at(vecs, i):
+        return jnp.broadcast_to(vecs[i // 8][i % 8:i % 8 + 1], (8, BLK))
+
+    for j in range(0, BASE, 2):
         gj, sj = divmod(j, 8)
-        pivot = jnp.broadcast_to(cols[j][gj][sj:sj + 1], (8, BLK))
-        inverse = 1.0 / pivot
-        scales[gj] = jnp.where(sub == sj, pivot, scales[gj])
-        ratio = [None] * groups
+        a, b, d = at(cols[j], j), at(cols[j], j + 1), at(cols[j + 1], j + 1)
+        det = a * d - b * b
+        ra = recip(a)
+        rdet = recip(det)
+        slope = b * ra
+        inv = a * rdet
+        scales[gj] = jnp.where(sub == sj, a, jnp.where(sub == sj + 1, det * ra, scales[gj]))
+        first, reduced, second = {}, {}, {}
         for g in range(gj, groups):
-            ratio[g] = cols[j][g] * inverse
+            c = cols[j][g]
+            first[g] = c * ra
+            reduced[g] = cols[j + 1][g] - c * slope
+            second[g] = reduced[g] * inv
             if g == gj:
-                ratio[g] = jnp.where(sub > sj, ratio[g], 0.0)
-        for k in range(j + 1, BASE):
-            row = jnp.broadcast_to(cols[k][gj][sj:sj + 1], (8, BLK))
-            for g in range(gj, groups):
-                if 8 * g + 7 > j:
-                    cols[k][g] = cols[k][g] - ratio[g] * row
-        row = jnp.broadcast_to(rows[gj][sj:sj + 1], (8, BLK))
+                first[g] = jnp.where(sub > sj + 1, first[g], 0.0)
+                second[g] = jnp.where(sub > sj + 1, second[g], 0.0)
+        for k in range(j + 2, BASE):
+            low, high = at(cols[j], k), at(reduced, k)
+            for g in range(k // 8, groups):
+                cols[k][g] = cols[k][g] - first[g] * low - second[g] * high
+        low = at(rows, j)
+        high = at(rows, j + 1) - slope * low
+        rows[gj] = jnp.where(sub == sj + 1, high, rows[gj])
         for g in range(gj, groups):
-            if 8 * g + 7 > j:
-                rows[g] = rows[g] - ratio[g] * row
-    done = jnp.concatenate([rows[g] * lax.rsqrt(scales[g]) for g in range(groups)], axis=0)
-    wide = lax.broadcasted_iota(jnp.int32, (BASE, BLK), 1)
-    below = jnp.where(wide >= r0 + BASE, done, 0.0)
-    update = tdot(below, done)
+            if 8 * g + 7 > j + 1:
+                rows[g] = rows[g] - first[g] * low - second[g] * high
+    return jnp.concatenate([rows[g] * lax.rsqrt(scales[g]) for g in range(groups)], axis=0)
+
+
+def factor_block(block, aside):
     rr = lax.broadcasted_iota(jnp.int32, (BLK, BLK), 0)
     cc = lax.broadcasted_iota(jnp.int32, (BLK, BLK), 1)
-    clear = (rr >= r0 + BASE) & (cc >= r0) & (cc < r0 + BASE)
-    tile[...] = jnp.where(clear, 0.0, tile[...]) - update
-    tile[pl.ds(r0, BASE), :] = done
-
-
-def inverse_kernel(n, scale, g_ref, x_ref, mat, tile):
+    diagonal = jnp.where(rr == cc, block, 0.0)
+    across = lax.rsqrt(jnp.sum(diagonal, axis=0, keepdims=True))
+    down = lax.rsqrt(jnp.sum(diagonal, axis=1, keepdims=True))
+    rest = block * across * down
+    parts = []
+    for p in range(BLK // BASE):
+        aside(p)
+        done = base_step(p, rest[:BASE])
+        parts.append(done)
+        if p + 1 < BLK // BASE:
+            r1 = (p + 1) * BASE
+            lane = lax.broadcasted_iota(jnp.int32, (BLK - r1, BLK), 1)
+            update = sdot(left_stack(done)[:, r1:], right_stack(done))
+            rest = jnp.where((lane >= r1 - BASE) & (lane < r1), 0.0, rest[BASE:]) - update
+    return jnp.where(cc <= rr, jnp.concatenate(parts, axis=0), 0.0) * across
+
+
+def rotate_kernel(states, scale, g_ref, z_ref, o_ref, mat, left, right, out, send, recv):
+    rows, n = z_ref.shape
     blocks = n // BLK
+    ms = lax.axis_index("state")
+    greet([{"state": lax.rem(ms + d, states)} for d in range(1, states)])
+    mine = pl.ds(pl.multiple_of(ms * rows, rows), rows)
+
+    def hand_over(t):
+        return remote(out.at[t], o_ref.at[mine], send.at[t], recv.at[ms], {"state": t})
+
+    def rotate_block(t):
+        strip = mat[at[t], :(t + 1) * BLK].astype(BF16)
+        block = lax.dot_general(
+            z_ref[:, :(t + 1) * BLK], strip, (((1,), (1,)), ((), ())), preferred_element_type=F32
+        ).astype(BF16)
+
+        @pl.when(ms == t)
+        def _():
+            o_ref[mine, :] = block
+
+        @pl.when(ms != t)
+        def _():
+            out[t] = block
+            hand_over(t).start()
+
+    at = [pl.ds(k * BLK, BLK) for k in range(blocks)]
     offset = 0
     for k in range(blocks):
         for j in range(k, blocks):
-            mat[k * BLK:(k + 1) * BLK, j * BLK:(j + 1) * BLK] = (
-                g_ref[offset * BLK:(offset + 1) * BLK, :] * scale
-            )
+            mat[at[k], at[j]] = g_ref[pl.ds(offset * BLK, BLK), :] * scale
             offset += 1
-    rr = lax.broadcasted_iota(jnp.int32, (BLK, BLK), 0)
-    cc = lax.broadcasted_iota(jnp.int32, (BLK, BLK), 1)
-
-    def step(k, carry):
-        rows = pl.ds(pl.multiple_of(k * BLK, BLK), BLK)
-        tile[...] = mat[rows, rows]
-
-        def inner(p, c):
-            base_step(p, tile)
-            return c
-
-        lax.fori_loop(0, BLK // BASE, inner, 0)
-        corner = jnp.where(cc <= rr, tile[...], 0.0)
-        mat[rows, rows] = (rr == cc).astype(F32)
-        mat[rows, :] = jnp.dot(corner, mat[rows, :], precision=HIGHEST, preferred_element_type=F32)
-
-        def update(i, c):
-            at = pl.ds(pl.multiple_of(i * BLK, BLK), BLK)
-            left = mat[rows, at]
-            mat[at, rows] = jnp.zeros((BLK, BLK), F32)
-            mat[at, :] = mat[at, :] - tdot(left, mat[rows, :])
-            return c
-
-        lax.fori_loop(k + 1, blocks, update, 0)
-        return carry
-
-    lax.fori_loop(0, blocks, step, 0)
+
+    def apply(k, i, diagonal):
+        slot = k % 2
+        if diagonal:
+            mat[at[i], at[i]] = mat[at[i], at[i]] - sdot(left[slot, :, at[i]], right[slot, :, at[i]])
+            return
+        lhs = left[slot, :, at[i]]
+        old = pl.ds(0, (k + 1) * BLK)
+        change = sdot(lhs, right[slot, :, old])
+        if k > 0:
+            done = pl.ds(0, k * BLK)
+            mat[at[i], done] = mat[at[i], done] - change[:, :k * BLK]
+        mat[at[i], at[k]] = -change[:, k * BLK:]
+        first = i + 1 if i == k + 1 else i
+        if first < blocks:
+            new = pl.ds(first * BLK, (blocks - first) * BLK)
+            mat[at[i], new] = mat[at[i], new] - sdot(lhs, right[slot, :, new])
+
     for k in range(blocks):
-        for j in range(blocks):
-            spot = (slice(k * BLK, (k + 1) * BLK), slice(j * BLK, (j + 1) * BLK))
-            if j > k:
-                x_ref[spot] = jnp.zeros((BLK, BLK), x_ref.dtype)
-            elif j < k:
-                x_ref[spot] = mat[spot].astype(x_ref.dtype)
-            else:
-                x_ref[spot] = jnp.where(cc <= rr, mat[spot], 0.0).astype(x_ref.dtype)
-
-
-def inverse_factor(packed, n, scale):
-    return pl.pallas_call(
-        functools.partial(inverse_kernel, n, scale),
-        out_shape=jax.ShapeDtypeStruct((n, n), BF16),
-        in_specs=[in_vmem()],
-        out_specs=in_vmem(),
-        scratch_shapes=[VMEM((n, n), F32), VMEM((BLK, BLK), F32)],
-        compiler_params=pltpu.CompilerParams(vmem_limit_bytes=40 * MIB),
-        cost_estimate=pl.CostEstimate(flops=6 * n**3, bytes_accessed=4 * n * n, transcendentals=0),
-    )(packed)
-
-
-def rotate_kernel(states, z_ref, x_ref, o_ref, out, send, recv):
-    rows, n = z_ref.shape
-    width = n // states
-    ms = lax.axis_index("state")
-    peers = [lax.rem(ms + d, states) for d in range(states)]
-    greet([{"state": peers[d]} for d in range(1, states)])
-    mine = pl.ds(pl.multiple_of(ms * rows, rows), rows)
-    copies = []
-    for d in list(range(1, states)) + [0]:
-        at = pl.ds(pl.multiple_of(peers[d] * width, width), width)
-        block = lax.dot_general(
-            z_ref[...], x_ref[at, :], (((1,), (1,)), ((), ())), preferred_element_type=F32
-        ).astype(BF16)
-        if d == 0:
-            o_ref[mine, :] = block
-        else:
-            out[d] = block
-            copies.append(remote(out.at[d], o_ref.at[mine], send.at[d], recv.at[d], {"state": peers[d]}))
-            copies[-1].start()
-    for c in copies:
-        c.wait()
-
-
-def rotate(rows, inverse, states):
+        def aside(p, k=k):
+            if k > 0:
+                todo = list(range(k, blocks))
+                for i in todo[p::BLK // BASE]:
+                    apply(k - 1, i, False)
+
+        corner = factor_block(mat[at[k], at[k]], aside)
+        mat[at[k], at[k]] = corner
+        lhs = left_stack(corner.T)
+        slot = k % 2
+        pieces = []
+        if k > 0:
+            done = pl.ds(0, k * BLK)
+            pieces.append((done, sdot(lhs, right_stack(mat[at[k], done]))))
+        if k + 1 < blocks:
+            new = pl.ds((k + 1) * BLK, (blocks - k - 1) * BLK)
+            pieces.append((new, sdot(lhs, right_stack(mat[at[k], new]))))
+            right[slot, :, at[k]] = right_stack(corner)
+        for where, piece in pieces:
+            mat[at[k], where] = piece
+            if k + 1 < blocks:
+                right[slot, :, where] = right_stack(piece)
+        if k + 1 < blocks:
+            left[slot, :, new] = left_stack(pieces[-1][1])
+            apply(k, k + 1, True)
+        rotate_block(k)
+    for t in range(states):
+
+        @pl.when(ms != t)
+        def _():
+            hand_over(t).wait_send()
+            rows_of = o_ref.at[pl.ds(t * rows, rows)]
+            remote(out.at[t], rows_of, send.at[t], recv.at[t], {"state": t}).wait_recv()
+
+
+def rotate(gram, rows, scale, states):
     count, n = rows.shape
     width = n // states
     return pl.pallas_call(
-        functools.partial(rotate_kernel, states),
+        functools.partial(rotate_kernel, states, scale),
         out_shape=jax.ShapeDtypeStruct((count * states, width), BF16),
         in_specs=[in_vmem(), in_vmem()],
         out_specs=in_vmem(),
         scratch_shapes=[
+            VMEM((n, n), F32),
+            VMEM((2, 6 * BLK, n), BF16),
+            VMEM((2, 6 * BLK, n), BF16),
             VMEM((states, count, width), BF16),
             pltpu.SemaphoreType.DMA((states,)),
             pltpu.SemaphoreType.DMA((states,)),
         ],
         compiler_params=pltpu.CompilerParams(
-            collective_id=2, has_side_effects=True, vmem_limit_bytes=40 * MIB
+            collective_id=2, has_side_effects=True, vmem_limit_bytes=48 * MIB
         ),
-        cost_estimate=pl.CostEstimate(flops=2 * count * n * n, bytes_accessed=4 * MIB, transcendentals=0),
-    )(rows, inverse)
+        cost_estimate=pl.CostEstimate(flops=2 * count * n * n + 6 * n**3, bytes_accessed=4 * MIB, transcendentals=0),
+    )(gram, rows)
 
 
 def on_device(coefficients, hamiltonian, neighbours, pattern):
@@ -498,8 +561,7 @@
     states = lax.axis_size("state")
     rows, gram = filter_and_gram(coefficients, hamiltonian, neighbours, pattern, elems, states)
     gram = sum_everywhere(gram)
-    inverse = inverse_factor(gram, states * width, 1.0 / (count * elems * basis))
-    result = rotate(rows, inverse, states)
+    result = rotate(gram, rows, 1.0 / (count * elems * basis), states)
     return result.reshape(count, basis, width)
 
 

time: 184 us -> 157 us (0.85)
  Pallas kernels: 178 us -> 149 us
    pallas_call x2 -> x1, Pallas kernels: 79.5 us -> 52 us  [rotate(): pl.pallas_call(functools.partial(rotate_kernel, states, scale), out_shape...]
    unnamed x7 -> x9, local copies, waits for them, and re-layouts: 5.93 us -> 5.76 us
where the time goes in v2:
time: 157 us; the launch traced here: 155 us
  Pallas kernels  149 us (95%)
  local copies, waits for them, and re-layouts  5.76 us (4%)
    pallas_call x1, Pallas kernels, sum_everywhere(): pl.pallas_call(sum_kernel, out_shape=jax.ShapeDtypeStruct(packed.shape, F...  59.2 us
    pallas_call x1, Pallas kernels, rotate(): pl.pallas_call(functools.partial(rotate_kernel, states, scale), out_shape...  52 us
    pallas_call x1, Pallas kernels, filter_and_gram(): pl.pallas_call(functools.partial(filter_kernel, elems, states), out_shape...  38.1 us
    unnamed x9, local copies, waits for them, and re-layouts  5.76 us

profile of v2, /device:TPU:1, one launch (start us, length us, event | category | flops | bytes accessed | tf_op | source)
XLA Modules:
  0.0 155.1 jit_solution(4333993086011242175)
XLA Ops:
  0.0 0.0 copy-start
  0.0 2.2 %copy-done = bf16[64,64,448]{2,1,0:T(8,128)(2,1)S(1)} copy-done((bf16[64,64,448]{2,1,0:T(8,128)(2,1)S(1)}, bf16[64,64,448]{2,1,0:T(8,128)(2,1)}, u32[]{:S(2)}) %copy-start) | copy-done | bytes 3670040
  2.2 0.0 copy-start.1
  2.2 1.2 copy-done.1
  3.4 0.0 copy-start.2
  3.4 0.7 copy-done.2
  4.1 0.0 copy-start.3
  4.1 0.7 copy-done.3
  4.8 38.1 %shard_map.46 = (bf16[512,1024]{1,0:T(8,128)(2,1)S(1)}, f32[4608,128]{1,0:T(8,128)S(1)}) custom-call(s32[6,64]{1,0:T(8,128)S(1)} %bitcast.4, s32[6,64]{1,0:T(8,128)S(1)} %bitcast.5, bf16[64,64,128]{2,1,0:T(8,128)(2,1)S(1)} %copy-done.1, bf16[64,64,448]{2,1,0:T(8,128)(2,1)S(1)} %copy-done), custom_call_target="tpu_custom_call" | custom-call | flops 2000000000 | bytes 8388608 | tf_op jit(solution)/shard_map/pallas_call | solution.py:162
  42.9 59.2 %shard_map.47.g_ref = f32[4608,128]{1,0:T(8,128)S(1)} custom-call(f32[4608,128]{1,0:T(8,128)S(1)} %get-tuple-element.7.src), custom_call_target="tpu_custom_call" | custom-call | flops 10000000 | bytes 5242880 | tf_op jit(solution)/shard_map/pallas_call | solution.py:329
  102.1 52.0 %shard_map.48 = bf16[4096,128]{1,0:T(8,128)(2,1)S(1)} custom-call(f32[4608,128]{1,0:T(8,128)S(1)} %shard_map.47.g_ref, bf16[512,1024]{1,0:T(8,128)(2,1)S(1)} %get-tuple-element.8.z_ref), custom_call_target="tpu_custom_call" | custom-call | flops 7516192768 | bytes 4194304 | tf_op jit(solution)/shard_map/pallas_call | solution.py:538
  154.1 1.0 copy.6
Async XLA Ops:
  0.0 2.2 %copy-start = (bf16[64,64,448]{2,1,0:T(8,128)(2,1)S(1)}, bf16[64,64,448]{2,1,0:T(8,128)(2,1)}, u32[]{:S(2)}) copy-start(bf16[64,64,448]{2,1,0:T(8,128)(2,1)} %h_hbm.1) | copy-start | bytes 11010052
  2.2 1.2 copy-start.1
  3.4 0.7 copy-start.2
  4.1 0.7 copy-start.3

commit v3 on v0

v3 whole, which is shorter than its diff:
```python
import functools

import jax
import jax.numpy as jnp
from jax import lax
from jax.experimental import pallas as pl
from jax.experimental.pallas import tpu as pltpu
from jax.sharding import PartitionSpec as P

LAYER = 32
CENTER = 0.5
HALF_WIDTH = 2.0
BLK = 128
BASE = 32
F32 = jnp.float32
BF16 = jnp.bfloat16
MESH = pl.DeviceIdType.MESH
VMEM = pltpu.VMEM
MIB = 1024 * 1024


def in_vmem():
    return pl.BlockSpec(memory_space=pltpu.VMEM)


def in_hbm():
    return pl.BlockSpec(memory_space=pl.ANY)


def in_smem():
    return pl.BlockSpec(memory_space=pltpu.SMEM)


def greet(devices):
    barrier = pltpu.get_barrier_semaphore()
    for device in devices:
        pl.semaphore_signal(barrier, inc=1, device_id=device, device_id_type=MESH)
    pl.semaphore_wait(barrier, len(devices))


def remote(src, dst, send, recv, device):
    return pltpu.make_async_remote_copy(
        src_ref=src, dst_ref=dst, send_sem=send, recv_sem=recv, device_id=device, device_id_type=MESH
    )


def recip(x):
    q = pl.reciprocal(x, approx=True)
    return q * (2.0 - x * q)


def split(x):
    h = x.astype(BF16)
    r = x - h.astype(F32)
    m = r.astype(BF16)
    return h, m, (r - m.astype(F32)).astype(BF16)


def left_stack(x):
    h, m, l = split(x)
    return jnp.concatenate([h, h, m, h, m, l], axis=0)


def right_stack(x):
    h, m, l = split(x)
    return jnp.concatenate([h, m, h, l, m, h], axis=0)


def sdot(a, b):
    return lax.dot_general(a, b, (((0,), (0,)), ((), ())), preferred_element_type=F32)


def base_step(p, panel):
    r0 = p * BASE
    lane = lax.broadcasted_iota(jnp.int32, (8, BLK), 1)
    sub = lax.broadcasted_iota(jnp.int32, (8, BLK), 0)
    groups = BASE // 8
    rows = [panel[8 * g:8 * g + 8] for g in range(groups)]
    cols = [
        {g: jnp.broadcast_to(rows[g][:, r0 + k:r0 + k + 1], (8, BLK)) for g in range(k // 8, groups)}
        for k in range(BASE)
    ]
    inside = (lane >= r0) & (lane < r0 + BASE)
    rows = [
        jnp.where(inside, (lane - r0 == sub + 8 * g).astype(F32), rows[g]) for g in range(groups)
    ]
    scales = [jnp.ones((8, BLK), F32) for _ in range(groups)]

    def at(vecs, i):
        return jnp.broadcast_to(vecs[i // 8][i % 8:i % 8 + 1], (8, BLK))

    for j in range(0, BASE, 2):
        gj, sj = divmod(j, 8)
        a, b, d = at(cols[j], j), at(cols[j], j + 1), at(cols[j + 1], j + 1)
        det = a * d - b * b
        ra = recip(a)
        rdet = recip(det)
        slope = b * ra
        inv = a * rdet
        scales[gj] = jnp.where(sub == sj, a, jnp.where(sub == sj + 1, det * ra, scales[gj]))
        first, reduced, second = {}, {}, {}
        for g in range(gj, groups):
            c = cols[j][g]
            first[g] = c * ra
            reduced[g] = cols[j + 1][g] - c * slope
            second[g] = reduced[g] * inv
            if g == gj:
                first[g] = jnp.where(sub > sj + 1, first[g], 0.0)
                second[g] = jnp.where(sub > sj + 1, second[g], 0.0)
        for k in range(j + 2, BASE):
            low, high = at(cols[j], k), at(reduced, k)
            for g in range(k // 8, groups):
                cols[k][g] = cols[k][g] - first[g] * low - second[g] * high
        low = at(rows, j)
        high = at(rows, j + 1) - slope * low
        rows[gj] = jnp.where(sub == sj + 1, high, rows[gj])
        for g in range(gj, groups):
            if 8 * g + 7 > j + 1:
                rows[g] = rows[g] - first[g] * low - second[g] * high
    return jnp.concatenate([rows[g] * lax.rsqrt(scales[g]) for g in range(groups)], axis=0)


def factor_block(block, aside):
    rr = lax.broadcasted_iota(jnp.int32, (BLK, BLK), 0)
    cc = lax.broadcasted_iota(jnp.int32, (BLK, BLK), 1)
    diagonal = jnp.where(rr == cc, block, 0.0)
    across = lax.rsqrt(jnp.sum(diagonal, axis=0, keepdims=True))
    down = lax.rsqrt(jnp.sum(diagonal, axis=1, keepdims=True))
    rest = block * across * down
    parts = []
    for p in range(BLK // BASE):
        aside(p)
        done = base_step(p, rest[:BASE])
        parts.append(done)
        if p + 1 < BLK // BASE:
            r1 = (p + 1) * BASE
            lane = lax.broadcasted_iota(jnp.int32, (BLK - r1, BLK), 1)
            update = sdot(left_stack(done)[:, r1:], right_stack(done))
            rest = jnp.where((lane >= r1 - BASE) & (lane < r1), 0.0, rest[BASE:]) - update
    return jnp.where(cc <= rr, jnp.concatenate(parts, axis=0), 0.0) * across


FIRST = (
    [(0, j) for j in range(8)],
    [(1, j) for j in range(1, 8)] + [(2, 2)],
)
SECOND = (
    [(2, j) for j in range(3, 8)] + [(3, j) for j in range(3, 8)],
    [(i, j) for i in range(4, 8) for j in range(i, 8)],
)
HALF = (len(FIRST[0]) + len(SECOND[0])) * BLK
STREAM_ROWS = (len(FIRST[0]) * BLK, len(SECOND[0]) * BLK)
STREAM_AT = (0, STREAM_ROWS[0])
SIZES = (4, 4, 8)
TILE = 8
WIDE = STREAM_ROWS[1] // 8


def packed_blocks():
    return FIRST[0] + SECOND[0] + FIRST[1] + SECOND[1]


def runs(pairs):
    found = []
    for i, j in pairs:
        if found and found[-1][0] == i and found[-1][1] + found[-1][2] == j:
            found[-1][2] += 1
        else:
            found.append([i, j, 1])
    return found


def whole_kernel(
    elems, states, scale, nbr, pat, v_hbm, h_hbm, o_ref,
    z_ref, res, mat, left_terms, right_terms, out, send, recv,
    v_ref, h_ref, load, acc, f_ref, y_ref, tail_a, head_a, tail_b, head_b,
    halo_send, halo_recv, swap_send, swap_recv,
    gram, pair, buf_a, buf_b, buf_c, buf_d,
    core_send, core_recv, up_send, up_recv, down_send, down_recv,
):
    count, basis, width = v_ref.shape
    rows = count * basis // states
    per = count // states
    me = lax.axis_index("elem")
    ms = lax.axis_index("state")
    right = lax.rem(me + 1, elems)
    left = lax.rem(me + elems - 1, elems)
    core = lax.rem(me, 2)
    place = [lax.rem(ms, 4), (ms // 4) * 2 + me // 16, lax.rem(me, 16) // 2]

    def device(dim, at, c):
        spot = list(place)
        if dim is not None:
            spot[dim] = at
        x, y, z = spot
        return {"elem": lax.rem(y, 2) * 16 + z * 2 + c, "state": (y // 2) * 4 + x}

    def peer(dim, d):
        return lax.rem(place[dim] + d, SIZES[dim])

    load_v = pltpu.make_async_copy(v_hbm, v_ref, load.at[0])
    load_h = pltpu.make_async_copy(h_hbm, h_ref, load.at[1])
    load_v.start()
    load_h.start()
    greet(
        [{"elem": right}, {"elem": left}]
        + [{"state": lax.rem(ms + d, states)} for d in range(1, states)]
        + [device(1, peer(1, d), core) for d in (1, 3)]
        + [device(2, peer(2, d), core) for d in range(1, 8)]
    )

    halo = ((tail_a, head_a), (tail_b, head_b))

    def exchange(stage, src):
        tail = remote(
            src.at[pl.ds(count - LAYER, LAYER)], halo[stage][0],
            halo_send.at[stage, 0], halo_recv.at[stage, 0], {"elem": right},
        )
        head = remote(
            src.at[pl.ds(0, LAYER)], halo[stage][1],
            halo_send.at[stage, 1], halo_recv.at[stage, 1], {"elem": left},
        )
        return tail, head

    def local_part(src):
        def body(e, carry):
            parts = [src[e]]
            for f in range(6):
                n = nbr[f, e]
                w = (pat[f, e] * (n // count == me).astype(jnp.int32)).astype(F32)
                parts.append(src[lax.rem(n, count)] * jnp.full((basis, width), w, F32).astype(BF16))
            stacked = jnp.concatenate(parts, axis=0)
            acc[e] = jnp.dot(h_ref[e], stacked, preferred_element_type=F32)
            return carry

        lax.fori_loop(0, count, body, 0, unroll=4)

    def image(stage, e, layer):
        face = 0 if layer == 1 else 1
        side = 1 if layer == 1 else 0
        w = pat[face, e].astype(F32)
        block = halo[stage][side][lax.rem(nbr[face, e], LAYER)]
        block = block * jnp.full((basis, width), w, F32).astype(BF16)
        strip = h_ref[e, :, (1 + face) * basis:(2 + face) * basis]
        return acc[e] + jnp.dot(strip, block, preferred_element_type=F32)

    load_v.wait()
    first = exchange(0, v_ref)
    for c in first:
        c.start()
    load_h.wait()
    local_part(v_ref)
    second = exchange(1, f_ref)
    for layer in range(2):
        first[layer].wait_recv()

        def one(i, carry):
            e = layer * LAYER + i
            f_ref[e] = ((image(0, e, layer) - CENTER * v_ref[e].astype(F32)) / HALF_WIDTH).astype(BF16)
            return carry

        lax.fori_loop(0, LAYER, one, 0, unroll=4)
        second[1 - layer].start()
    local_part(f_ref)

    def swap(t, source):
        lanes = pl.ds(pl.multiple_of(source * width, width), width)
        return remote(
            y_ref.at[pl.ds(t * rows, rows)], z_ref.at[:, lanes],
            swap_send.at[t], swap_recv.at[source], {"state": t},
        )

    for layer in range(2):
        second[layer].wait_recv()

        def two(i, carry):
            e = layer * LAYER + i
            out = 2.0 * (image(1, e, layer) - CENTER * f_ref[e].astype(F32)) / HALF_WIDTH
            y_ref[pl.ds(pl.multiple_of(e * basis, basis), basis), :] = (out - v_ref[e].astype(F32)).astype(BF16)
            return carry

        lax.fori_loop(0, LAYER, two, 0, unroll=4)
        for t in range(layer * states // 2, (layer + 1) * states // 2):

            @pl.when(ms != t)
            def _():
                swap(t, ms).start()

    z_ref[:, pl.ds(pl.multiple_of(ms * width, width), width)] = y_ref[
        pl.ds(pl.multiple_of(ms * rows, rows), rows), :
    ]
    for c in first + second:
        c.wait_send()
    for t in range(states):

        @pl.when(ms != t)
        def _():
            swap(t, t).wait_recv()

    other = device(None, None, 1 - core)
    mine = pl.multiple_of(core * HALF, TILE)
    theirs = pl.multiple_of((1 - core) * HALF, TILE)

    def product(half, stream):
        at = half * HALF + STREAM_AT[stream]
        for i, j, n in runs((FIRST, SECOND)[stream][half]):
            strip = lax.dot_general(
                z_ref[:, i * BLK:(i + 1) * BLK], z_ref[:, j * BLK:(j + n) * BLK],
                (((0,), (0,)), ((), ())), preferred_element_type=F32,
            )
            for b in range(n):
                gram[at:at + BLK, :] = strip[:, b * BLK:(b + 1) * BLK]
                at += BLK

    def hand(stream):
        spot = pl.ds(STREAM_AT[stream], STREAM_ROWS[stream])
        return remote(
            gram.at[pl.ds(theirs + STREAM_AT[stream], STREAM_ROWS[stream])], pair.at[spot],
            core_send.at[stream], core_recv.at[stream], other,
        )

    for c in range(2):

        @pl.when(core == c)
        def _():
            for stream in range(2):
                product(1 - c, stream)
                hand(stream).start()
            for stream in range(2):
                product(c, stream)

    def ds(start, length):
        return pl.ds(pl.multiple_of(start, TILE), length)

    length_a = [STREAM_ROWS[s] // 8 for s in range(2)]
    length_b = [STREAM_ROWS[s] // 32 for s in range(2)]
    start_0 = [[mine + STREAM_AT[s] + p * STREAM_ROWS[s] // 2 for p in range(2)] for s in range(2)]
    start_a = [[start_0[s][p] + place[p] * length_a[s] for p in range(2)] for s in range(2)]
    start_b = [[start_a[s][p] + place[1 - p] * length_b[s] for p in range(2)] for s in range(2)]
    started = []

    def launch(copies):
        for c in copies:
            c.start()
        started.extend(copies)
        return copies

    def scatter(level, s):
        length = (length_a, length_b)[level][s]
        copies = []
        for d in range(1, 4):
            for p in range(2):
                dim = p if level == 0 else 1 - p
                to = peer(dim, d)
                start = (start_0, start_a)[level][s][p] + to * length
                copies.append(
                    remote(
                        gram.at[ds(start, length)], (buf_a, buf_b)[level].at[s, p, d, pl.ds(0, length)],
                        up_send.at[level, s, p, d], up_recv.at[level, s, p, d], device(dim, to, core),
                    )
                )
        return launch(copies)

    def gather_sums(level, s, copies):
        length = (length_a, length_b)[level][s]
        for c in copies:
            c.wait_recv()
        for p in range(2):
            own = ds((start_a, start_b)[level][s][p], length)
            total = gram[own, :]
            for d in range(1, 4):
                total = total + (buf_a, buf_b)[level][s, p, d, pl.ds(0, length), :]
            gram[own, :] = total

    def tile_of(s, z):
        return start_b[s][0] + (z // 4) * (start_b[s][1] - start_b[s][0]) + lax.rem(z, 4) * TILE

    def scatter_z(s):
        copies = []
        for d in range(1, 8):
            to = peer(2, d)
            copies.append(
                remote(
                    gram.at[ds(tile_of(s, to), TILE)], buf_c.at[s, d],
                    up_send.at[2, s, 0, d], up_recv.at[2, s, 0, d], device(2, to, core),
                )
            )
        if s == 1:
            for p in range(2):
                spare = ds(start_b[1][p] + 4 * TILE, TILE)
                buf_d[place[2], p] = gram[spare, :]
            for d in range(1, 8):
                copies.append(
                    remote(
                        buf_d.at[place[2]], buf_d.at[place[2]],
                        up_send.at[2, s, 1, d], up_recv.at[2, s, 1, d], device(2, peer(2, d), core),
                    )
                )
        return launch(copies)

    def finish_z(s, copies):
        for c in copies:
            c.wait_recv()
        own = ds(tile_of(s, place[2]), TILE)
        total = gram[own, :]
        for d in range(1, 8):
            total = total + buf_c[s, d]
        res[own, :] = total
        if s == 1:
            for p in range(2):
                total = buf_d[0, p]
                for z in range(1, 8):
                    total = total + buf_d[z, p]
                res[ds(start_b[1][p] + 4 * TILE, TILE), :] = total

    def spread_z(s):
        own = ds(tile_of(s, place[2]), TILE)
        return launch([
            remote(
                res.at[own], res.at[own], down_send.at[2, s, 0, d], down_recv.at[2, s, 0, d],
                device(2, peer(2, d), core),
            )
            for d in range(1, 8)
        ])

    def spread(level, s):
        copies = []
        for d in range(1, 4):
            for p in range(2):
                dim = p if level == 0 else 1 - p
                own = ds((start_a, start_b)[level][s][p], (length_a, length_b)[level][s])
                copies.append(
                    remote(
                        res.at[own], res.at[own], down_send.at[level, s, p, d], down_recv.at[level, s, p, d],
                        device(dim, peer(dim, d), core),
                    )
                )
        return launch(copies)

    def arrived(copies):
        for c in copies:
            c.wait_recv()

    def give(s):
        own = ds(mine + STREAM_AT[s], STREAM_ROWS[s])
        return launch([remote(res.at[own], res.at[own], core_send.at[2 + s], core_recv.at[2 + s], other)])

    stage = [None, None]
    for s in range(2):
        hand(s).wait_recv()
        own = ds(mine + STREAM_AT[s], STREAM_ROWS[s])
        gram[own, :] = gram[own, :] + pair[pl.ds(STREAM_AT[s], STREAM_ROWS[s]), :]
        stage[s] = scatter(0, s)
    for s in range(2):
        gather_sums(0, s, stage[s])
        stage[s] = scatter(1, s)
        if s == 0:
            gather_sums(1, s, stage[s])
            stage[s] = scatter_z(s)
    gather_sums(1, 1, stage[1])
    stage[1] = scatter_z(1)
    for s in range(2):
        finish_z(s, stage[s])
        stage[s] = spread_z(s)
    for s in range(2):
        arrived(stage[s])
        stage[s] = spread(1, s)
    for s in range(2):
        arrived(stage[s])
        stage[s] = spread(0, s)
    arrived(stage[0])
    stage[0] = give(0)

    blocks = states * width // BLK
    at = [pl.ds(k * BLK, BLK) for k in range(blocks)]
    early = set(FIRST[0] + FIRST[1])
    own_rows = pl.ds(pl.multiple_of(ms * rows, rows), rows)

    def unpack(wanted):
        for spot, (i, j) in enumerate(packed_blocks()):
            if ((i, j) in early) == wanted:
                mat[at[i], at[j]] = res[spot * BLK:(spot + 1) * BLK, :] * scale

    def hand_over(t):
        return remote(out.at[t], o_ref.at[own_rows], send.at[t], recv.at[ms], {"state": t})

    def rotate_block(t):
        strip = mat[at[t], :(t + 1) * BLK].astype(BF16)
        block = lax.dot_general(
            z_ref[:, :(t + 1) * BLK], strip, (((1,), (1,)), ((), ())), preferred_element_type=F32
        ).astype(BF16)

        @pl.when(ms == t)
        def _():
            o_ref[own_rows, :] = block

        @pl.when(ms != t)
        def _():
            out[t] = block
            hand_over(t).start()

    def apply(k, i, diagonal, known=False):
        slot = k % 2
        if diagonal:
            mat[at[i], at[i]] = mat[at[i], at[i]] - sdot(left_terms[slot, :, at[i]], right_terms[slot, :, at[i]])
            return
        lhs = left_terms[slot, :, at[i]]
        old = pl.ds(0, (k + 1) * BLK)
        change = sdot(lhs, right_terms[slot, :, old])
        if k > 0:
            done = pl.ds(0, k * BLK)
            mat[at[i], done] = mat[at[i], done] - change[:, :k * BLK]
        mat[at[i], at[k]] = -change[:, k * BLK:]
        first = i + 1 if known else i
        if first < blocks:
            new = pl.ds(first * BLK, (blocks - first) * BLK)
            mat[at[i], new] = mat[at[i], new] - sdot(lhs, right_terms[slot, :, new])

    for k in range(blocks):
        if k == 0:
            arrived(stage[0])
            unpack(True)
        if k == 1:
            arrived(stage[1])
            stage[1] = give(1)
        if k == 2:
            arrived(stage[1])
            unpack(False)
        todo = [[(k - 1, i, i == k)] for i in range(k, blocks)]
        if k == 0:
            todo = []
        elif k == 1:
            todo = todo[:1]
        elif k == 2:
            todo = [[(0, i, i == 2), (1, i, i == 2)] for i in range(2, blocks)]

        def aside(p, todo=todo):
            for group in todo[p::BLK // BASE]:
                for source, i, known in group:
                    apply(source, i, False, known)

        corner = factor_block(mat[at[k], at[k]], aside)
        mat[at[k], at[k]] = corner
        lhs = left_stack(corner.T)
        slot = k % 2
        pieces = []
        if k > 0:
            done = pl.ds(0, k * BLK)
            pieces.append((done, sdot(lhs, right_stack(mat[at[k], done]))))
        if k + 1 < blocks:
            new = pl.ds((k + 1) * BLK, (blocks - k - 1) * BLK)
            pieces.append((new, sdot(lhs, right_stack(mat[at[k], new]))))
            right_terms[slot, :, at[k]] = right_stack(corner)
        for where, piece in pieces:
            mat[at[k], where] = piece
            if k + 1 < blocks:
                right_terms[slot, :, where] = right_stack(piece)
        if k + 1 < blocks:
            left_terms[slot, :, new] = left_stack(pieces[-1][1])
            apply(k, k + 1, True)
        if k == 0:
            apply(0, 2, True)
        rotate_block(k)
    for t in range(states):

        @pl.when(ms != t)
        def _():
            hand_over(t).wait_send()
            rows_of = o_ref.at[pl.ds(t * rows, rows)]
            remote(out.at[t], rows_of, send.at[t], recv.at[t], {"state": t}).wait_recv()
    for c in started:
        c.wait_send()
    for s in range(2):
        hand(s).wait_send()
    for t in range(states):

        @pl.when(ms != t)
        def _():
            swap(t, ms).wait_send()


def whole(coefficients, hamiltonian, neighbours, pattern, elems, states):
    count, basis, width = coefficients.shape
    rows = count * basis // states
    n = states * width
    scale = 1.0 / (count * elems * basis)
    dma = pltpu.SemaphoreType.DMA
    return pl.pallas_call(
        functools.partial(whole_kernel, elems, states, scale),
        out_shape=jax.ShapeDtypeStruct((count * basis, width), BF16),
        in_specs=[in_smem(), in_smem(), in_hbm(), in_hbm()],
        out_specs=in_vmem(),
        scratch_shapes=[
            VMEM((rows, n), BF16),
            VMEM((2 * HALF, BLK), F32),
            VMEM((n, n), F32),
            VMEM((2, 6 * BLK, n), BF16),
            VMEM((2, 6 * BLK, n), BF16),
            VMEM((states, rows, width), BF16),
            dma((states,)),
            dma((states,)),
            VMEM(coefficients.shape, BF16),
            VMEM(hamiltonian.shape, BF16),
            dma((2,)),
            VMEM((count, basis, width), F32),
            VMEM((count, basis, width), BF16),
            VMEM((count * basis, width), BF16),
            VMEM((LAYER, basis, width), BF16),
            VMEM((LAYER, basis, width), BF16),
            VMEM((LAYER, basis, width), BF16),
            VMEM((LAYER, basis, width), BF16),
            dma((2, 2)),
            dma((2, 2)),
            dma((states,)),
            dma((states,)),
            VMEM((2 * HALF, BLK), F32),
            VMEM((HALF, BLK), F32),
            VMEM((2, 2, 4, WIDE, BLK), F32),
            VMEM((2, 2, 4, WIDE // 4, BLK), F32),
            VMEM((2, 8, TILE, BLK), F32),
            VMEM((8, 2, TILE, BLK), F32),
            dma((4,)),
            dma((4,)),
            dma((3, 2, 2, 8)),
            dma((3, 2, 2, 8)),
            dma((3, 2, 2, 8)),
            dma((3, 2, 2, 8)),
        ],
        compiler_params=pltpu.CompilerParams(
            collective_id=0, has_side_effects=True, vmem_limit_bytes=60 * MIB
        ),
        cost_estimate=pl.CostEstimate(flops=12 * 10**9, bytes_accessed=8 * MIB, transcendentals=0),
    )(neighbours.T, pattern.T, coefficients, hamiltonian)


def on_device(coefficients, hamiltonian, neighbours, pattern):
    count, basis, width = coefficients.shape
    elems = lax.axis_size("elem")
    states = lax.axis_size("state")
    result = whole(coefficients, hamiltonian, neighbours, pattern, elems, states)
    return result.reshape(count, basis, width)


def solution(mesh):
    return jax.shard_map(
        on_device,
        mesh=mesh,
        in_specs=(
            P("elem", None, "state"),
            P("elem", None, None),
            P("elem", None),
            P("elem", None),
        ),
        out_specs=P("elem", None, "state"),
        check_vma=False,
    )
```

time: 882 us -> 135 us (0.15)
  waiting for transfers between devices: 440 us -> 0 us
  other arithmetic: 288 us -> 0 us
  Pallas kernels: 0 us -> 131 us
  local copies, waits for them, and re-layouts: 62 us -> 2.26 us
  matrix products: 57.1 us -> 0 us
  between operations: 18.8 us -> 0.01 us
    another operation x34 -> x0, other arithmetic: 256 us -> none  [the longest x30 173 us: on_device(): factor = jnp.linalg.cholesky(gram_matrix)]
    psum x1 -> x0, waiting for transfers between devices: 222 us -> none  [on_device(): column_sum = lax.psum(partial_value, 'elem')]
    all_gather x2 -> x0, waiting for transfers between devices: 205 us -> none  [the longest x1 128 us: on_device(): all_states = lax.all_gather(rows_local, 'state', axis=1, tiled=True)]
    pallas_call x0 -> x1, Pallas kernels: none -> 131 us  [whole(): pl.pallas_call(functools.partial(whole_kernel, elems, states, scale), out...]
    another operation x29 -> x0, matrix products: 35.5 us -> none  [the longest x14 23.1 us: on_device(): factor = jnp.linalg.cholesky(gram_matrix)]
    gather x2 -> x0, local copies, waits for them, and re-layouts: 26.7 us -> none  [apply_hamiltonian(): gathered = padded[slots] * weights]
    another operation x36 -> x0, local copies, waits for them, and re-layouts: 26 us -> none
    dot_general x4 -> x0, matrix products: 21.6 us -> none  [the longest x2 9.12 us: apply_hamiltonian(): jnp.einsum('eik,eks->eis', hamilton, stacked, preferred_element_type=jnp....]
  transfers between devices with their start and end apart: 7 -> 0, of which waited for: 7 -> 0; matrix products, arithmetic and copies ran while one was open for 0% -> 0% of each run, Pallas kernels for 0% -> 0%
where the time goes in v3:
time: 135 us; the launch traced here: 133 us
  Pallas kernels  131 us (97%)
  local copies, waits for them, and re-layouts  2.26 us (2%)
    pallas_call x1, Pallas kernels, whole(): pl.pallas_call(functools.partial(whole_kernel, elems, states, scale), out...  131 us

profile of v3, /device:TPU:1, one launch (start us, length us, event | category | flops | bytes accessed | tf_op | source)
XLA Modules:
  0.0 132.8 jit_solution(2554498269887610342)
XLA Ops:
  0.0 130.5 %shard_map.46 = bf16[4096,128]{1,0:T(8,128)(2,1)} custom-call(s32[6,64]{1,0:T(8,128)} %bitcast.4, s32[6,64]{1,0:T(8,128)} %bitcast.5, bf16[64,64,128]{2,1,0:T(8,128)(2,1)} %v_hbm.1, bf16[64,64,448]{2,1,0:T(8,128)(2,1)} %h_hbm.1), custom_call_target="tpu_custom_call" | custom-call | flops 12000000000 | bytes 8388608 | tf_op jit(solution)/shard_map/pallas_call | solution.py:588
  130.5 2.3 %copy.6 = bf16[64,64,128]{2,1,0:T(8,128)(2,1)} copy(bf16[64,64,128]{2,1,0:T(8,128)(2,1)} %bitcast.3) | data formatting | bytes 2097152

commit v4 on v3

--- a/solution.py
+++ b/solution.py
@@ -251,7 +251,7 @@
     load_h.wait()
     local_part(v_ref)
     second = exchange(1, f_ref)
-    for layer in range(2):
+    def stage_one(layer):
         first[layer].wait_recv()
 
         def one(i, carry):
@@ -261,6 +261,14 @@
 
         lax.fori_loop(0, LAYER, one, 0, unroll=4)
         second[1 - layer].start()
+
+    for c in range(2):
+
+        @pl.when(core == c)
+        def _():
+            stage_one(1 - c)
+            stage_one(c)
+
     local_part(f_ref)
 
     def swap(t, source):
@@ -270,7 +278,7 @@
             swap_send.at[t], swap_recv.at[source], {"state": t},
         )
 
-    for layer in range(2):
+    def stage_two(layer):
         second[layer].wait_recv()
 
         def two(i, carry):
@@ -285,6 +293,13 @@
             @pl.when(ms != t)
             def _():
                 swap(t, ms).start()
+
+    for c in range(2):
+
+        @pl.when(core == c)
+        def _():
+            stage_two(1 - c)
+            stage_two(c)
 
     z_ref[:, pl.ds(pl.multiple_of(ms * width, width), width)] = y_ref[
         pl.ds(pl.multiple_of(ms * rows, rows), rows), :
@@ -486,18 +501,34 @@
 
     def rotate_block(t):
         strip = mat[at[t], :(t + 1) * BLK].astype(BF16)
-        block = lax.dot_general(
+        out[t] = lax.dot_general(
             z_ref[:, :(t + 1) * BLK], strip, (((1,), (1,)), ((), ())), preferred_element_type=F32
         ).astype(BF16)
 
+    def send_block(t):
         @pl.when(ms == t)
         def _():
-            o_ref[own_rows, :] = block
+            o_ref[own_rows, :] = out[t]
 
         @pl.when(ms != t)
         def _():
-            out[t] = block
             hand_over(t).start()
+
+    def rest_of_panel(k):
+        slot = k % 2
+        lhs = left_stack(mat[at[k], at[k]].T)
+        places = [pl.ds(0, k * BLK)] if k > 0 else []
+        if k + 2 < blocks:
+            places.append(pl.ds((k + 2) * BLK, (blocks - k - 2) * BLK))
+        for where in places:
+            piece = sdot(lhs, right_stack(mat[at[k], where]))
+            mat[at[k], where] = piece
+            if k + 1 < blocks:
+                right_terms[slot, :, where] = right_stack(piece)
+        if k + 1 < blocks:
+            right_terms[slot, :, at[k]] = right_stack(mat[at[k], at[k]])
+        if k + 2 < blocks:
+            left_terms[slot, :, where] = left_stack(piece)
 
     def apply(k, i, diagonal, known=False):
         slot = k % 2
@@ -534,33 +565,33 @@
         elif k == 2:
             todo = [[(0, i, i == 2), (1, i, i == 2)] for i in range(2, blocks)]
 
-        def aside(p, todo=todo):
-            for group in todo[p::BLK // BASE]:
+        def aside(p, k=k, todo=todo):
+            if p == 0 and k > 0:
+                rest_of_panel(k - 1)
+                return
+            if p == 1 and k > 0:
+                rotate_block(k - 1)
+            if p == 2 and k == 1:
+                apply(0, 2, True)
+            for group in todo[max(p - 1, 0)::BLK // BASE - 1]:
                 for source, i, known in group:
                     apply(source, i, False, known)
 
         corner = factor_block(mat[at[k], at[k]], aside)
         mat[at[k], at[k]] = corner
-        lhs = left_stack(corner.T)
-        slot = k % 2
-        pieces = []
         if k > 0:
-            done = pl.ds(0, k * BLK)
-            pieces.append((done, sdot(lhs, right_stack(mat[at[k], done]))))
+            send_block(k - 1)
         if k + 1 < blocks:
-            new = pl.ds((k + 1) * BLK, (blocks - k - 1) * BLK)
-            pieces.append((new, sdot(lhs, right_stack(mat[at[k], new]))))
-            right_terms[slot, :, at[k]] = right_stack(corner)
-        for where, piece in pieces:
-            mat[at[k], where] = piece
-            if k + 1 < blocks:
-                right_terms[slot, :, where] = right_stack(piece)
-        if k + 1 < blocks:
-            left_terms[slot, :, new] = left_stack(pieces[-1][1])
+            slot = k % 2
+            piece = sdot(left_stack(corner.T), right_stack(mat[at[k], at[k + 1]]))
+            mat[at[k], at[k + 1]] = piece
+            right_terms[slot, :, at[k + 1]] = right_stack(piece)
+            left_terms[slot, :, at[k + 1]] = left_stack(piece)
             apply(k, k + 1, True)
-        if k == 0:
-            apply(0, 2, True)
-        rotate_block(k)
+        else:
+            rest_of_panel(k)
+            rotate_block(k)
+            send_block(k)
     for t in range(states):
 
         @pl.when(ms != t)

time: 135 us -> 133 us (0.985)
  Pallas kernels: 131 us -> 129 us
    pallas_call x1, Pallas kernels: 131 us -> 129 us  [whole(): pl.pallas_call(functools.partial(whole_kernel, elems, states, scale), out...]
where the time goes in v4:
time: 133 us; the launch traced here: 131 us
  Pallas kernels  129 us (97%)
  local copies, waits for them, and re-layouts  2.26 us (2%)
    pallas_call x1, Pallas kernels, whole(): pl.pallas_call(functools.partial(whole_kernel, elems, states, scale), out...  129 us

profile of v4, /device:TPU:1, one launch (start us, length us, event | category | flops | bytes accessed | tf_op | source)
XLA Modules:
  0.0 131.2 jit_solution(15855746080527253204)
XLA Ops:
  0.0 128.9 %shard_map.46 = bf16[4096,128]{1,0:T(8,128)(2,1)} custom-call(s32[6,64]{1,0:T(8,128)} %bitcast.4, s32[6,64]{1,0:T(8,128)} %bitcast.5, bf16[64,64,128]{2,1,0:T(8,128)(2,1)} %v_hbm.1, bf16[64,64,448]{2,1,0:T(8,128)(2,1)} %h_hbm.1), custom_call_target="tpu_custom_call" | custom-call | flops 12000000000 | bytes 8388608 | tf_op jit(solution)/shard_map/pallas_call | solution.py:619
  128.9 2.3 %copy.6 = bf16[64,64,128]{2,1,0:T(8,128)(2,1)} copy(bf16[64,64,128]{2,1,0:T(8,128)(2,1)} %bitcast.3) | data formatting | bytes 2097152
